TPU v7x, 256 devices: a whole 4x4x8 slice. The times are simulated.
256 devices in a mesh: wide: 16 (over z, core), narrow: 16 (over y, x).
Axes of the slice: x: 4, y: 4, z: 8, core: 2. Of those that a mesh axis runs over, the one named last changes fastest.
Arguments:
- histories: bfloat16 [16, 16, 1024, 256], P('wide', 'narrow')
- lengths: int32 [16, 16, 4], P('wide', 'narrow'), may hold values from 0 to 1024, as said below
- w_in: bfloat16 [256, 1024], replicated, may hold values from -0.375 to 0.375
- w_out: bfloat16 [256, 256], replicated, may hold values from -0.375 to 0.375
- item_table: float32 [524288, 256], P(('wide', 'narrow'))
- neg_blocks: int32 [16, 64], P('wide'), may hold values from 0 to 4095, as said below
- targets: int32 [16, 16, 512], P('wide'), may hold values from 0 to 524287, as said below
Outputs:
- losses: float32 [16, 16, 512], P('wide', 'narrow')
- item_grad: float32 [524288, 256], P(('wide', 'narrow'))
Inputs may be any that keep to these rules, and one draw needn't show every extreme that they name: Each device's lengths sum to at most 1024; the sums of the 16 devices with one narrow index add up to 16 * 512, and one of them is exactly 1024; some device holds one history of exactly 1024 slots. `neg_blocks`: row w lists 64 distinct blocks, each held by a device of wide index w (block b is item rows b * 128 to b * 128 + 127, held by device b // 16 of wide+narrow), exactly 64 // 16 from each such device. targets[w, n, j] is an item row of one of the blocks in neg_blocks[w].
All inputs are finite; a program needn't handle non-finite values.
Results may differ from a plain program's by a relative error of at most 0.0043.
Values may be sent and summed in bfloat16 or wider, within the bound.
A program may use at most 128 MiB of HBM per device.

v0:
```python
import jax
import jax.numpy as jnp
from jax import lax
from jax.sharding import PartitionSpec as P

D = 256
HEADS = 2
DH = 128
BLOCK = 128


logit_scale = 20.0


def unit_rows(rows):
    return (
        rows
        * lax.rsqrt(jnp.mean(rows * rows, axis=-1, keepdims=True) + 1e-06)
        * rows.shape[-1] ** (-0.5)
    )


def encode(history, lengths_dev, w_in, w_out):
    slots = history.shape[0]
    width = w_out.shape[0]
    projected = jax.nn.silu(jnp.dot(history, w_in, preferred_element_type=jnp.float32)).astype(
        jnp.bfloat16
    )
    gate_u = projected[:, :width]
    values = projected[:, width : 2 * width].reshape(slots, HEADS, DH)
    query = projected[:, 2 * width : 3 * width].reshape(slots, HEADS, DH)
    keys_h = projected[:, 3 * width :].reshape(slots, HEADS, DH)
    places = jnp.arange(slots, dtype=jnp.int32)
    ends = jnp.cumsum(lengths_dev)
    segment = jnp.sum((places[:, None] >= ends[None, :]).astype(jnp.int32), axis=1)
    seq_start = jnp.max(jnp.where(ends[None, :] <= places[:, None], ends[None, :], 0), axis=1)
    counts = (places - seq_start + 1).astype(jnp.float32)
    allowed = (segment[:, None] == segment[None, :]) & (places[None, :] <= places[:, None])
    scores = jnp.einsum("ihd,jhd->hij", query, keys_h, preferred_element_type=jnp.float32)
    weights = (
        jnp.where(allowed[None], jax.nn.silu(scores * DH ** (-0.5)), 0.0) / counts[None, :, None]
    )
    weights = weights.astype(jnp.bfloat16)
    attended = jnp.einsum(
        "hij,jhd->ihd", weights, values, preferred_element_type=jnp.float32
    ).reshape(slots, width)
    average = jnp.mean(attended, axis=-1, keepdims=True)
    spread = jnp.mean((attended - average) ** 2, axis=-1, keepdims=True)
    mixed = ((attended - average) * lax.rsqrt(spread + 1e-05) * gate_u.astype(jnp.float32)).astype(
        jnp.bfloat16
    )
    state = history.astype(jnp.float32) + jnp.dot(mixed, w_out, preferred_element_type=jnp.float32)
    live = places < ends[-1]
    return jnp.where(live[:, None], unit_rows(state), 0.0).astype(jnp.bfloat16)


def scores_of(token_rows, cand_rows):
    return logit_scale * jnp.einsum(
        "td,cd->tc", token_rows, cand_rows, preferred_element_type=jnp.float32
    )


def local(histories, lengths, w_in, w_out, item_table, neg_blocks, targets):
    history = histories[0, 0]
    slots_dev = history.shape[0]
    encoded = encode(history, lengths[0, 0], w_in, w_out)
    wide_count = lax.axis_size("wide")
    wide_rank = lax.axis_index("wide")
    group_count = lax.axis_size("narrow")
    group_rank = lax.axis_index("narrow")
    all_lengths = lax.all_gather(lengths, "wide", axis=0, tiled=True)
    totals = jnp.sum(all_lengths[:, 0, :], axis=1)
    ends = jnp.cumsum(totals)
    starts = ends - totals
    tok_bal = targets.shape[2]
    lane_ids = jnp.arange(wide_count, dtype=jnp.int32)
    stream_pos = jnp.arange(tok_bal, dtype=jnp.int32) * wide_count + wide_rank
    source = jnp.sum((ends[None, :] <= stream_pos[:, None]).astype(jnp.int32), axis=1)
    source_start = jnp.sum(
        jnp.where(lane_ids[None, :] == source[:, None], starts[None, :], 0), axis=1
    )
    inner = stream_pos - source_start
    whole = lax.all_gather(encoded, "wide", axis=0, tiled=True)
    balanced = whole[source * slots_dev + inner]
    blocks = neg_blocks[0]
    blk_count = blocks.shape[0]
    per_owner = blk_count // group_count
    table_blocks = item_table.shape[0] // BLOCK
    first_block = (wide_rank * group_count + group_rank) * table_blocks
    owner_lane = blocks // table_blocks - wide_rank * group_count
    order = jnp.argsort(owner_lane * blk_count + jnp.arange(blk_count, dtype=jnp.int32))
    sorted_blocks = blocks[order]
    own_blocks = (
        lax.dynamic_slice_in_dim(sorted_blocks, group_rank * per_owner, per_owner) - first_block
    )
    raw = item_table.reshape(table_blocks, BLOCK, D)[own_blocks].reshape(per_owner * BLOCK, D)
    own_units = unit_rows(raw).astype(jnp.bfloat16)
    my_targets = lax.dynamic_index_in_dim(targets[0], group_rank, 0, keepdims=False)
    cands = lax.all_gather(own_units, "narrow", axis=0, tiled=True)
    cand_total = cands.shape[0]
    block_match = sorted_blocks[None, :] == (my_targets // BLOCK)[:, None]
    rank_of = jnp.sum(
        jnp.where(block_match, jnp.arange(blk_count, dtype=jnp.int32)[None, :], 0), axis=1
    )
    hit_col = rank_of * BLOCK + my_targets % BLOCK
    span = min(cand_total, 2048)
    sumexp = jnp.zeros((tok_bal,), jnp.float32)
    positive = jnp.zeros((tok_bal,), jnp.float32)
    for piece in range(cand_total // span):
        logits = scores_of(balanced, cands[piece * span : (piece + 1) * span])
        col_ids = piece * span + jnp.arange(span, dtype=jnp.int32)
        sumexp = sumexp + jnp.sum(jnp.exp(logits), axis=1)
        positive = positive + jnp.sum(
            jnp.where(col_ids[None, :] == hit_col[:, None], logits, 0.0), axis=1
        )
    losses = jnp.log(sumexp) - positive
    logits = scores_of(balanced, cands)
    col_ids = jnp.arange(per_owner * BLOCK * lax.axis_size("narrow"), dtype=jnp.int32)
    hit = (col_ids[None, :] == hit_col[:, None]).astype(jnp.float32)
    slope = (jnp.exp(logits) / sumexp[:, None] - hit).astype(jnp.bfloat16)
    grads = lax.psum_scatter(
        logit_scale * jnp.dot(slope.T, balanced, preferred_element_type=jnp.float32),
        "narrow",
        scatter_dimension=0,
        tiled=True,
    )
    _, pull = jax.vjp(unit_rows, raw)
    own_grad = pull(grads)[0]
    item_grad = (
        jnp.zeros((table_blocks, BLOCK, D), jnp.float32)
        .at[own_blocks]
        .set(own_grad.reshape(per_owner, BLOCK, D))
    )
    return (losses[None, None, :], item_grad.reshape(table_blocks * BLOCK, D))


def solution(mesh):
    in_specs = (
        P("wide", "narrow", None, None),
        P("wide", "narrow", None),
        P(),
        P(),
        P(("wide", "narrow"), None),
        P("wide", None),
        P("wide", None, None),
    )
    out_specs = (P("wide", "narrow", None), P(("wide", "narrow"), None))
    return jax.shard_map(local, mesh=mesh, in_specs=in_specs, out_specs=out_specs, check_vma=False)
```

profile of v0, /device:TPU:2, one launch (start us, length us, event | category | flops | bytes accessed | tf_op | source)
XLA Modules:
  0.0 268.4 jit_solution(8270508282247542242)
XLA Ops:
  7.2 0.0 all-gather.3.cloned.1.call-start
  7.2 2.2 copy.24
  9.4 2.5 multiply_convert_fusion
  12.0 1.3 copy-done.3
  13.3 1.2 fusion.26
  14.5 0.2 reduce-window.12
  14.7 0.6 slice.28
  15.3 0.1 convert_reduce_fusion.1
  15.4 1.6 fusion
  17.0 6.7 %fusion.27 = (f32[1024]{0:T(1024)S(1)}, f32[2,128,1024]{2,1,0:T(8,128)S(1)}) fusion(bf16[1024,2,128]{0,2,1:T(8,128)(2,1)} %bitcast.86, f32[1024]{0:T(1024)S(1)} %add_convert_fusion, pred[1024,1024]{1,0:T(8,128)(4,1)} %fusion, bf16[1024,2,128]{0,2,1:T(8,128)(2,1)} %bitcast.85, bf16[1024,2,128]{0,2,1:T(8,128)(2,1)} %bitcast.84), kind=kOutput, calls=%fused_computation.99 | convolution fusion | flops 1090780160 | bytes 3678208 | tf_op jit(solution)/shard_map/hij,jhd->ihd/dot_general | solution.py:44
  23.7 0.1 fusion.16
  23.8 1.3 fusion.14
  25.1 1.4 multiply_reduce_fusion
  26.5 0.7 iota_compare_fusion.6
  27.2 0.9 select_convert_fusion
  28.1 0.0 all-gather.3.cloned.1.call-update
  28.1 0.0 all-gather.5.cloned.1.call-start
  28.2 2.0 sort.17
  30.3 0.8 gather_fusion.1
  31.1 0.1 compare_select_fusion.1
  31.1 0.6 gather_fusion.2
  31.7 0.1 multiply_reduce_fusion.1
  31.9 0.8 fusion.19
  32.8 0.0 reduce-scatter.2.cloned.1.call-start
  32.8 20.0 %all_gather.10 = s32[16,1,4]{2,1,0:T(1,128)S(1)} all-gather(s32[1,1,4]{2,1,0:T(1,128)S(1)} %copy-done.5), channel_id=1, replica_groups=mesh['wide'=16,'narrow'=16] {'wide'}, dimensions={0}, use_global_device_ids=true | all-gather | bytes 272 | tf_op jit(solution)/shard_map/all_gather | solution.py:71
  52.8 0.4 reduce_sum.176
  53.2 0.1 copy.27
  53.3 0.1 reduce.5
  53.5 0.7 constant_dynamic-slice_fusion
  54.2 0.1 convert_reduce_fusion
  54.3 0.1 select_reduce_fusion.5
  54.5 0.1 select_reduce_fusion.4
  54.6 32.6 %all-gather.3.cloned.1.call-done = bf16[16384,256]{0,1:T(8,128)(2,1)} async-done(((bf16[1024,256]{0,1:T(8,128)(2,1)}), bf16[16384,256]{0,1:T(8,128)(2,1)}) %all-gather.3.cloned.1.call-update) | async-done | bytes 8388624 | tf_op jit(solution)/shard_map/all_gather | solution.py:83
  87.2 11.9 %copy.28 = bf16[16384,256]{1,0:T(8,128)(2,1)} copy(bf16[16384,256]{0,1:T(8,128)(2,1)} %all-gather.3.cloned.1.call-done) | data formatting | bytes 16777216 | tf_op jit(solution)/shard_map/all_gather | solution.py:83
  99.1 6.3 %gather_fusion = bf16[512,256]{1,0:T(8,128)(2,1)S(1)} fusion(bf16[16384,256]{1,0:T(8,128)(2,1)} %copy.28, s32[1024]{0:T(1024)S(1)} %pad_clamp_fusion.2), kind=kCustom, calls=%fused_computation | custom fusion | bytes 526336 | tf_op jit(solution)/shard_map/gather | solution.py:84
  105.4 39.4 %all-gather.5.cloned.1.call-done = bf16[8192,256]{1,0:T(8,128)(2,1)} async-done(((bf16[512,256]{1,0:T(8,128)(2,1)}), bf16[8192,256]{1,0:T(8,128)(2,1)}) %all-gather.5.cloned.1.call-update) | async-done | bytes 4194320 | tf_op jit(solution)/shard_map/all_gather | solution.py:99
  144.7 2.1 fusion.10
  146.9 0.4 copy-done.2
  147.2 0.7 fusion.4
  148.0 0.7 fusion.6
  148.7 4.8 %exponential_reduce_fusion.2 = (f32[512]{0:T(512)S(1)}, f32[512]{0:T(512)S(1)}, f32[512]{0:T(512)S(1)}, f32[512]{0:T(512)S(1)}, f32[512]{0:T(512)S(1)}, /*index=...) fusion(s32[512]{0:T(512)S(1)} %fusion.21, s32[2048]{0:T(1024)S(1)} %iota_add_fusion.2, s32[2048]{0:T(1024)S(1)} %get-tuple-element.32, ...), kind=kOutput, calls=%fused_computation.15 | convolution fusion | flops 557838336 | bytes 13936640 | tf_op jit(solution)/shard_map/td,cd->tc/dot_general | solution.py:58
  153.6 0.6 add_subtract_fusion
  154.2 11.1 %convolution_multiply_fusion = f32[8192,256]{1,0:T(8,128)} fusion(bf16[512,256]{1,0:T(8,128)(2,1)S(1)} %gather_fusion, bf16[8192,256]{1,0:T(8,128)(2,1)} %all-gather.5.cloned.1.call-done, s32[512]{0:T(512)S(1)} %fusion.21, f32[512]{0:T(512)S(1)} %get-tuple-element.15), kind=kOutput, calls=%fused_computation.6 | convolution fusion | flops 4322230272 | bytes 12849152 | tf_op jit(solution)/shard_map/dot_general | solution.py:122
  165.3 90.0 %reduce-scatter.2.cloned.1.call-done = f32[512,256]{1,0:T(8,128)} async-done(((f32[8192,256]{1,0:T(8,128)}), f32[512,256]{1,0:T(8,128)}) %reduce-scatter.2.cloned.1.call-update) | async-done | bytes 524304 | tf_op jit(solution)/shard_map/reduce_scatter | solution.py:121
  255.4 1.2 fusion.20
  256.6 1.3 add_add_fusion
  257.9 1.5 broadcast_in_dim.128
  259.4 2.5 scatter_fusion
  (33 shorter events, 0.2 us)
Async XLA Ops:
  7.2 24.0 %copy-start = (f32[2048,256]{1,0:T(8,128)S(1)}, f32[2048,256]{1,0:T(8,128)}, u32[]{:S(2)}) copy-start(f32[2048,256]{1,0:T(8,128)} %param.11) | copy-start | bytes 6291460
  7.2 80.0 %all-gather.3.cloned.1.call-start = ((), (), s32[]{:S(2)}) async-start(), calls=%async_computation.1 | async-start | bytes 8912896 | tf_op jit(solution)/shard_map/all_gather | solution.py:83
  9.4 5.1 %copy-start.5 = (s32[1,1,4]{2,1,0:T(1,128)S(1)}, s32[1,1,4]{2,1,0:T(1,128)}, u32[]{:S(2)}) copy-start(s32[1,1,4]{2,1,0:T(1,128)} %param.8) | copy-start | bytes 52
  12.0 1.3 copy-start.3
  17.0 8.1 %copy-start.4 = (bf16[256,256]{1,0:T(8,128)(2,1)S(1)}, bf16[256,256]{1,0:T(8,128)(2,1)}, u32[]{:S(2)}) copy-start(bf16[256,256]{1,0:T(8,128)(2,1)} %param.10) | copy-start | bytes 393220
  23.6 4.5 %copy-start.1 = (s32[1,64]{1,0:T(1,128)S(1)}, s32[1,64]{1,0:T(1,128)}, u32[]{:S(2)}) copy-start(s32[1,64]{1,0:T(1,128)} %param.12) | copy-start | bytes 772
  28.1 116.6 %all-gather.5.cloned.1.call-start = ((), (), s32[]{:S(2)}) async-start(), calls=%async_computation.2 | async-start | bytes 4456448 | tf_op jit(solution)/shard_map/all_gather | solution.py:99
  32.8 222.6 %reduce-scatter.2.cloned.1.call-start = ((), (), s32[]{:S(2)}) async-start(), calls=%async_computation.3 | async-start | bytes 8912896 | tf_op jit(solution)/shard_map/reduce_scatter | solution.py:121
  144.7 2.5 copy-start.2
Sparse Core Ops, SparseCore 0:
  28.3 58.8 all-gather.2
  89.6 55.0 all-gather.4
  165.5 89.8 reduce-scatter.1
where the time goes:
time: 269 us; the launch traced here: 268 us
  waiting for transfers between devices  162 us (60%)
  local copies, waits for them, and re-layouts  30.1 us (11%)
  matrix products  30.1 us (11%)
  blocking collectives  20 us (7%)
  between operations  14 us (5%)
  other arithmetic  12 us (4%)
    reduce_scatter x1, waiting for transfers between devices, local(): lax.psum_scatter(logit_scale * jnp.dot(slope.T, balanced, preferred_eleme...  90 us
    all_gather x1, waiting for transfers between devices, local(): cands = lax.all_gather(own_units, 'narrow', axis=0, tiled=True)  39.4 us
    all_gather x1, waiting for transfers between devices, local(): whole = lax.all_gather(encoded, 'wide', axis=0, tiled=True)  32.6 us
    all_gather x1, blocking collectives, local(): all_lengths = lax.all_gather(lengths, 'wide', axis=0, tiled=True)  20 us
    all_gather x1, local copies, waits for them, and re-layouts, local(): whole = lax.all_gather(encoded, 'wide', axis=0, tiled=True)  11.9 us
    dot_general x1, matrix products, local(): jnp.dot(slope.T, balanced, preferred_element_type=jnp.float32)  11.1 us
    dot_general x4, matrix products, scores_of(): jnp.einsum('td,cd->tc', token_rows, cand_rows, preferred_element_type=jnp...  8.42 us
    dot_general x1, matrix products, encode(): jnp.einsum('hij,jhd->ihd', weights, values, preferred_element_type=jnp.fl...  6.65 us
  transfers between devices with their start and end apart: 3, of which 3 were waited for; matrix products, arithmetic and copies ran while one was open for 9% of the time, Pallas kernels for 0%

commit v1 on v0

v1 whole, which is shorter than its diff:
```python
import math

import jax
import jax.numpy as jnp
from jax import lax
from jax.experimental import pallas as pl
from jax.experimental.pallas import tpu as pltpu
from jax.sharding import PartitionSpec as P

D = 256
DH = 128
BLOCK = 128
GROUP = 16
SIDE = 4
SLOTS = 1024
TILE = 256
TILES = SLOTS // TILE
PART = TILE // GROUP
PAIR = SLOTS // GROUP
TOK = 512
CAND = 512
SCALE = 20.0
MESH = pl.DeviceIdType.MESH
F32 = jnp.float32
BF16 = jnp.bfloat16


def unit_scale(rows):
    return lax.rsqrt(jnp.mean(rows * rows, axis=-1, keepdims=True) + 1e-06)


def silu(x):
    half = 0.5 * x
    return half + half * jnp.tanh(half)


def prep_kernel(neg_ref, table_ref, units_ref, raw_ref, order_ref, counts, sems):
    wide = lax.axis_index("wide")
    narrow = lax.axis_index("narrow")
    for owner in range(GROUP):
        counts[owner] = 0

    @pl.loop(0, 64)
    def _(i):
        block = neg_ref[0, i]
        owner = lax.shift_right_logical(block, 4) - wide * GROUP
        seen = counts[owner]
        order_ref[owner * 4 + seen] = block
        counts[owner] = seen + 1

    first = (wide * GROUP + narrow) * 16
    copies = []
    for q in range(4):
        row = pl.multiple_of((order_ref[narrow * 4 + q] - first) * BLOCK, BLOCK)
        copy = pltpu.make_async_copy(
            table_ref.at[pl.ds(row, BLOCK)], raw_ref.at[pl.ds(q * BLOCK, BLOCK)], sems.at[q]
        )
        copy.start()
        copies.append(copy)
    for q in range(4):
        copies[q].wait()
        rows = raw_ref[pl.ds(q * BLOCK, BLOCK), :]
        units_ref[pl.ds(q * BLOCK, BLOCK), :] = (rows * unit_scale(rows) * 0.0625).astype(BF16)


def prep(neg_blocks, item_table):
    return pl.pallas_call(
        prep_kernel,
        out_shape=(
            jax.ShapeDtypeStruct((CAND, D), BF16),
            jax.ShapeDtypeStruct((CAND, D), F32),
            jax.ShapeDtypeStruct((64,), jnp.int32),
        ),
        in_specs=[pl.BlockSpec(memory_space=pltpu.SMEM), pl.BlockSpec(memory_space=pl.ANY)],
        out_specs=(
            pl.BlockSpec(memory_space=pltpu.VMEM),
            pl.BlockSpec(memory_space=pltpu.VMEM),
            pl.BlockSpec(memory_space=pltpu.SMEM),
        ),
        scratch_shapes=[pltpu.SMEM((GROUP,), jnp.int32), pltpu.SemaphoreType.DMA((4,))],
        compiler_params=pltpu.CompilerParams(vmem_limit_bytes=16 * 2**20),
        name="prep",
    )(neg_blocks, item_table)


def main_kernel(
    len_ref,
    order_ref,
    hist_ref,
    win_ref,
    wout_ref,
    units_ref,
    targets_ref,
    grad_ref,
    loss_ref,
    proj,
    tot,
    send,
    recv,
    tok,
    cand,
    expd,
    slope,
    sums,
    hits,
    gsend,
    grecv,
    tot_s,
    tot_r,
    a2a_s,
    a2a_r,
    cand_s,
    cand_r,
    tok_s,
    tok_r,
    sum_s,
    sum_r,
    hit_s,
    hit_r,
    g_s,
    g_r,
):
    me = lax.axis_index("wide")
    narrow = lax.axis_index("narrow")
    core = lax.rem(me, 2)
    tok_step = 4 - 3 * core
    cand_step = 1 + 3 * core
    my_t = lax.rem(narrow // tok_step, SIDE)
    my_c = lax.rem(narrow // cand_step, SIDE)

    def wide_peer(d):
        return (lax.rem(me + d, GROUP), narrow)

    def tok_peer(s):
        return (me, lax.rem(my_t + s, SIDE) * tok_step + my_c * cand_step)

    def cand_peer(s):
        return (me, my_t * tok_step + lax.rem(my_c + s, SIDE) * cand_step)

    def remote(src, dst, ssem, rsem, peer):
        return pltpu.make_async_remote_copy(
            src_ref=src, dst_ref=dst, send_sem=ssem, recv_sem=rsem, device_id=peer, device_id_type=MESH
        )

    barrier = pltpu.get_barrier_semaphore()
    for d in range(1, GROUP):
        pl.semaphore_signal(barrier, inc=1, device_id=wide_peer(d), device_id_type=MESH)
    for s in range(1, SIDE):
        pl.semaphore_signal(barrier, inc=1, device_id=tok_peer(s), device_id_type=MESH)
        pl.semaphore_signal(barrier, inc=1, device_id=cand_peer(s), device_id_type=MESH)

    e0 = len_ref[0, 0, 0]
    e1 = e0 + len_ref[0, 0, 1]
    e2 = e1 + len_ref[0, 0, 2]
    e3 = e2 + len_ref[0, 0, 3]
    tot[me] = jnp.full((8, 128), e3, jnp.int32)
    cand[my_c] = units_ref[...]
    pl.semaphore_wait(barrier, GROUP - 1 + 2 * (SIDE - 1))

    tot_copies = [remote(tot.at[me], tot.at[me], tot_s.at[d], tot_r.at[d], wide_peer(d)) for d in range(1, GROUP)]
    for copy in tot_copies:
        copy.start()
    cand_copies = [
        remote(units_ref, cand.at[my_c], cand_s.at[s], cand_r.at[s], cand_peer(s)) for s in range(1, SIDE)
    ]
    for copy in cand_copies:
        copy.start()

    for b in range(TILES):
        rows = pl.ds(b * TILE, TILE)
        x = jnp.dot(hist_ref[0, 0, rows, :], win_ref[...], preferred_element_type=F32)
        proj[rows, :] = silu(x).astype(BF16)

    lanes = lax.broadcasted_iota(jnp.int32, (TILE, TILE), 1)
    subs = lax.broadcasted_iota(jnp.int32, (TILE, TILE), 0)
    take = None
    for b in range(TILES):
        rows = pl.ds(b * TILE, TILE)
        place = subs + b * TILE
        start = jnp.maximum(
            jnp.maximum(jnp.where(place >= e0, e0, 0), jnp.where(place >= e1, e1, 0)),
            jnp.maximum(jnp.where(place >= e2, e2, 0), jnp.where(place >= e3, e3, 0)),
        )
        share = 1.0 / (place - start + 1).astype(F32)
        heads = []
        for h in range(2):
            q = proj[rows, pl.ds(512 + h * DH, DH)]
            total = jnp.zeros((TILE, DH), F32)
            for kb in range(b + 1):
                krows = pl.ds(kb * TILE, TILE)
                k = proj[krows, pl.ds(768 + h * DH, DH)]
                v = proj[krows, pl.ds(256 + h * DH, DH)]
                scores = lax.dot_general(q, k, (((1,), (1,)), ((), ())), preferred_element_type=F32)
                weights = silu(scores * (DH ** -0.5)) * share
                allowed = lanes + kb * TILE >= start
                if kb == b:
                    allowed = allowed & (lanes <= subs)
                weights = jnp.where(allowed, weights, 0.0).astype(BF16)
                total = total + jnp.dot(weights, v, preferred_element_type=F32)
            heads.append(total)
        attended = jnp.concatenate(heads, axis=1)
        centred = attended - jnp.mean(attended, axis=-1, keepdims=True)
        spread = jnp.mean(centred * centred, axis=-1, keepdims=True)
        gate = proj[rows, pl.ds(0, D)].astype(F32)
        mixed = (centred * lax.rsqrt(spread + 1e-05) * gate).astype(BF16)
        state = hist_ref[0, 0, rows, :].astype(F32) + jnp.dot(mixed, wout_ref[...], preferred_element_type=F32)
        encoded = jnp.where(place < e3, state * unit_scale(state) * 0.0625, 0.0).astype(BF16)
        if b == 0:
            for copy in tot_copies:
                copy.wait_recv()
            begin = jnp.zeros((8, 128), jnp.int32)
            for w in range(GROUP):
                begin = begin + jnp.where(w < me, tot[w], 0)
            begin = jnp.concatenate([begin[0:1, :]] * 2, axis=1)
            wanted = (subs & 15) * 16 + (((subs >> 4) - begin) & 15)
            take = (lanes == wanted).astype(F32).astype(BF16)
        packed = jnp.dot(take, encoded, preferred_element_type=F32).astype(BF16)
        send[b] = packed.reshape(GROUP, PART, D)
        for d in range(1, GROUP):
            dest = lax.rem(me + d, GROUP)
            remote(
                send.at[b, dest], recv.at[me, pl.ds(b * PART, PART)], a2a_s, a2a_r, wide_peer(d)
            ).start()
        recv[me, pl.ds(b * PART, PART), :] = send[b, me]

    pltpu.make_async_copy(recv.at[pl.ds(0, GROUP - 1)], recv.at[pl.ds(0, GROUP - 1)], a2a_r).wait()
    lane = lax.broadcasted_iota(jnp.int32, (1, 128), 1)
    slot = lax.broadcasted_iota(jnp.int32, (TOK, 128), 0)
    begin = jnp.zeros((1, 128), jnp.int32)
    pieces = []
    for w in range(0, GROUP, 2):
        second = begin + tot[w, 0:1, :]
        base = jnp.where(lane < PAIR, begin, second)
        goes_to = ((base - me + 15) >> 4) + (lane & (PAIR - 1))
        pieces.append((slot == goes_to).astype(F32).astype(BF16))
        begin = second + tot[w + 1, 0:1, :]
    gather = jnp.concatenate(pieces, axis=1)
    tok[my_t] = jnp.dot(gather, recv[...].reshape(GROUP * PAIR, D), preferred_element_type=F32).astype(BF16)

    tok_copies = [
        remote(tok.at[my_t], tok.at[my_t], tok_s.at[s], tok_r.at[s], tok_peer(s)) for s in range(1, SIDE)
    ]
    for copy in tok_copies:
        copy.start()
    for copy in cand_copies:
        copy.wait_recv()

    row8 = lax.broadcasted_iota(jnp.int32, (8, TOK), 0)
    part = jnp.zeros((8, TOK), F32)
    for s in (0, 1, 3, 2):
        if s:
            tok_copies[s - 1].wait_recv()
        t = lax.rem(my_t + SIDE - s, SIDE)

        def forward(c, total):
            scores = lax.dot_general(
                cand[c], tok[t], (((1,), (1,)), ((), ())), preferred_element_type=F32
            )
            value = jnp.exp2(scores * (SCALE * math.log2(math.e)))
            expd[t, pl.ds(pl.multiple_of(c * CAND, CAND), CAND), :] = value
            return total + jnp.sum(value.reshape(CAND // 8, 8, TOK), axis=0)

        total = lax.fori_loop(0, SIDE, forward, jnp.zeros((8, TOK), F32))
        part = jnp.where(row8 == t, jnp.sum(total, axis=0, keepdims=True), part)
    sums[my_t] = part
    sum_copies = [
        remote(sums.at[my_t], sums.at[my_t], sum_s.at[s], sum_r.at[s], tok_peer(s)) for s in range(1, SIDE)
    ]
    for copy in sum_copies:
        copy.start()
    for copy in sum_copies:
        copy.wait_recv()
    sumexp = (sums[0] + sums[1]) + (sums[2] + sums[3])
    inverse = 1.0 / sumexp

    offset = lax.broadcasted_iota(jnp.int32, (BLOCK, TOK), 0)
    hit_part = jnp.zeros((8, TOK), F32)
    g_copies = []
    own = None
    for s in (1, 3, 2, 0):
        c = lax.rem(my_c + s, SIDE)
        owner = my_t * tok_step + c * cand_step
        for t in range(SIDE):
            target = targets_ref[0, pl.ds(t * tok_step + my_c * cand_step, 1), :]
            scale_t = inverse[t : t + 1, :]

            def backward(q, total):
                at = pl.multiple_of(c * CAND + q * BLOCK, BLOCK)
                value = expd[t, pl.ds(at, BLOCK), :]
                hit = offset == target - order_ref[owner * 4 + q] * BLOCK
                grad = value * scale_t - jnp.where(hit, 1.0, 0.0)
                slope[pl.ds(pl.multiple_of(q * BLOCK, BLOCK), BLOCK), pl.ds(t * TOK, TOK)] = grad.astype(BF16)
                found = jnp.where(hit, value, 0.0)
                return total + jnp.sum(found.reshape(BLOCK // 8, 8, TOK), axis=0)

            found = lax.fori_loop(0, 4, backward, jnp.zeros((8, TOK), F32))
            hit_part = hit_part + jnp.where(row8 == t, jnp.sum(found, axis=0, keepdims=True), 0.0)
        grads = SCALE * jnp.dot(slope[...], tok[...].reshape(SIDE * TOK, D), preferred_element_type=F32)
        if s:
            gsend[s] = grads.astype(BF16)
            copy = remote(gsend.at[s], grecv.at[s], g_s.at[s], g_r.at[s], cand_peer(s))
            copy.start()
            g_copies.append(copy)
        else:
            grad_ref[...] = grads
    hits[my_t] = hit_part
    hit_copies = [
        remote(hits.at[my_t], hits.at[my_t], hit_s.at[s], hit_r.at[s], tok_peer(s)) for s in range(1, SIDE)
    ]
    for copy in hit_copies:
        copy.start()
    for copy in hit_copies:
        copy.wait_recv()
    found = (hits[0] + hits[1]) + (hits[2] + hits[3])
    loss = jnp.where(row8 == my_t, jnp.log(sumexp) - jnp.log(found), 0.0)
    loss_ref[...] = jnp.sum(loss, axis=0, keepdims=True)
    for copy in g_copies:
        copy.wait_recv()
    grad_ref[...] += (grecv[1].astype(F32) + grecv[2].astype(F32)) + grecv[3].astype(F32)

    for copy in tot_copies + cand_copies + tok_copies + sum_copies + hit_copies + g_copies:
        copy.wait_send()
    pltpu.make_async_copy(recv.at[pl.ds(0, GROUP - 1)], recv.at[pl.ds(0, GROUP - 1)], a2a_s).wait()


def main(lengths, order, histories, w_in, w_out, units, targets):
    dma = pltpu.SemaphoreType.DMA
    vmem = pl.BlockSpec(memory_space=pltpu.VMEM)
    smem = pl.BlockSpec(memory_space=pltpu.SMEM)
    return pl.pallas_call(
        main_kernel,
        out_shape=(jax.ShapeDtypeStruct((CAND, D), F32), jax.ShapeDtypeStruct((1, TOK), F32)),
        in_specs=[smem, smem, vmem, vmem, vmem, vmem, vmem],
        out_specs=(vmem, vmem),
        scratch_shapes=[
            pltpu.VMEM((SLOTS, 4 * D), BF16),
            pltpu.VMEM((GROUP, 8, 128), jnp.int32),
            pltpu.VMEM((TILES, GROUP, PART, D), BF16),
            pltpu.VMEM((GROUP, PAIR, D), BF16),
            pltpu.VMEM((SIDE, TOK, D), BF16),
            pltpu.VMEM((SIDE, CAND, D), BF16),
            pltpu.VMEM((SIDE, SIDE * CAND, TOK), F32),
            pltpu.VMEM((CAND, SIDE * TOK), BF16),
            pltpu.VMEM((SIDE, 8, TOK), F32),
            pltpu.VMEM((SIDE, 8, TOK), F32),
            pltpu.VMEM((SIDE, CAND, D), BF16),
            pltpu.VMEM((SIDE, CAND, D), BF16),
            dma((GROUP,)),
            dma((GROUP,)),
            dma,
            dma,
        ]
        + [dma((SIDE,))] * 10,
        compiler_params=pltpu.CompilerParams(
            collective_id=0, has_side_effects=True, vmem_limit_bytes=48 * 2**20
        ),
        name="main",
    )(lengths, order, histories, w_in, w_out, units, targets)


def finish_kernel(order_ref, grad_ref, raw_ref, loss_in, out_ref, loss_ref):
    wide = lax.axis_index("wide")
    narrow = lax.axis_index("narrow")
    first = (wide * GROUP + narrow) * 16
    loss_ref[...] = loss_in[...]
    out_ref[...] = jnp.zeros_like(out_ref)
    for q in range(4):
        rows = raw_ref[pl.ds(q * BLOCK, BLOCK), :]
        grad = grad_ref[pl.ds(q * BLOCK, BLOCK), :]
        scale = unit_scale(rows)
        along = jnp.mean(rows * grad, axis=-1, keepdims=True)
        value = (grad - rows * (scale * scale * along)) * (scale * 0.0625)
        at = pl.multiple_of((order_ref[narrow * 4 + q] - first) * BLOCK, BLOCK)
        out_ref[pl.ds(at, BLOCK), :] = value


def finish(order, grads, raw, loss):
    vmem = pl.BlockSpec(memory_space=pltpu.VMEM)
    return pl.pallas_call(
        finish_kernel,
        out_shape=(jax.ShapeDtypeStruct((16 * BLOCK, D), F32), jax.ShapeDtypeStruct((1, TOK), F32)),
        in_specs=[pl.BlockSpec(memory_space=pltpu.SMEM), vmem, vmem, vmem],
        out_specs=(vmem, vmem),
        compiler_params=pltpu.CompilerParams(vmem_limit_bytes=16 * 2**20),
        name="finish",
    )(order, grads, raw, loss)


def local(histories, lengths, w_in, w_out, item_table, neg_blocks, targets):
    units, raw, order = prep(neg_blocks, item_table)
    grads, loss = main(lengths, order, histories, w_in, w_out, units, targets)
    item_grad, loss = finish(order, grads, raw, loss)
    return (loss[None], item_grad)


def solution(mesh):
    in_specs = (
        P("wide", "narrow", None, None),
        P("wide", "narrow", None),
        P(),
        P(),
        P(("wide", "narrow"), None),
        P("wide", None),
        P("wide", None, None),
    )
    out_specs = (P("wide", "narrow", None), P(("wide", "narrow"), None))
    return jax.shard_map(local, mesh=mesh, in_specs=in_specs, out_specs=out_specs, check_vma=False)
```

time: 269 us -> 68.2 us (0.25)
  waiting for transfers between devices: 162 us -> 0 us
  Pallas kernels: 0 us -> 64.8 us
  matrix products: 30.1 us -> 0 us
  local copies, waits for them, and re-layouts: 30.1 us -> 2.26 us
  blocking collectives: 20 us -> 0 us
  between operations: 14 us -> 0.71 us
  other arithmetic: 12 us -> 0 us
    reduce_scatter x1 -> x0, waiting for transfers between devices: 90 us -> none  [local(): lax.psum_scatter(logit_scale * jnp.dot(slope.T, balanced, preferred_eleme...]
    all_gather x2 -> x0, waiting for transfers between devices: 72 us -> none  [the longest x1 39.4 us: local(): cands = lax.all_gather(own_units, 'narrow', axis=0, tiled=True)]
    pallas_call x0 -> x3, Pallas kernels: none -> 64.8 us  [the longest x1 59.8 us: main(): pl.pallas_call(main_kernel, out_shape=(jax.ShapeDtypeStruct((CAND, D), F3...]
    dot_general x8 -> x0, matrix products: 30.1 us -> none  [the longest x1 11.1 us: local(): jnp.dot(slope.T, balanced, preferred_element_type=jnp.float32)]
    all_gather x1 -> x0, blocking collectives: 20 us -> none  [local(): all_lengths = lax.all_gather(lengths, 'wide', axis=0, tiled=True)]
    all_gather x1 -> x0, local copies, waits for them, and re-layouts: 11.9 us -> none  [local(): whole = lax.all_gather(encoded, 'wide', axis=0, tiled=True)]
    gather x3 -> x0, local copies, waits for them, and re-layouts: 7.66 us -> none  [the longest x1 6.3 us: local(): balanced = whole[source * slots_dev + inner]]
    convert_element_type x4 -> x0, other arithmetic: 3.04 us -> none  [the longest x1 1.26 us: encode(): ((attended - average) * lax.rsqrt(spread + 1e-05) * gate_u.astype(jnp.flo...]
  transfers between devices with their start and end apart: 3 -> 0, of which waited for: 3 -> 0; matrix products, arithmetic and copies ran while one was open for 9% -> 0% of each run, Pallas kernels for 0% -> 0%
where the time goes in v1:
time: 68.2 us; the launch traced here: 67.8 us
  Pallas kernels  64.8 us (95%)
  local copies, waits for them, and re-layouts  2.26 us (3%)
  between operations  0.71 us (1%)
    pallas_call x1, Pallas kernels, main(): pl.pallas_call(main_kernel, out_shape=(jax.ShapeDtypeStruct((CAND, D), F3...  59.8 us
    pallas_call x1, Pallas kernels, prep(): pl.pallas_call(prep_kernel, out_shape=(jax.ShapeDtypeStruct((CAND, D), BF...  2.8 us
    unnamed x14, local copies, waits for them, and re-layouts  2.26 us
    pallas_call x1, Pallas kernels, finish(): pl.pallas_call(finish_kernel, out_shape=(jax.ShapeDtypeStruct((16 * BLOCK...  2.21 us

profile of v1, /device:TPU:2, one launch (start us, length us, event | category | flops | bytes accessed | tf_op | source)
XLA Modules:
  0.0 67.8 jit_solution(6422230364451794623)
XLA Ops:
  0.6 0.0 copy-start
  0.6 1.6 %copy-done = f32[2048,256]{1,0:T(8,128)S(1)} copy-done((f32[2048,256]{1,0:T(8,128)S(1)}, f32[2048,256]{1,0:T(8,128)}, u32[]{:S(2)}) %copy-start) | copy-done | bytes 2097176
  2.2 0.0 copy-start.6
  2.2 0.7 copy-done.6
  2.9 0.0 copy-start.1
  2.9 0.0 copy-start.2
  2.9 0.0 copy-start.3
  2.9 0.0 copy-start.4
  2.9 0.0 copy-start.5
  2.9 2.8 %prep.1 = (bf16[512,256]{1,0:T(8,128)(2,1)S(1)}, f32[512,256]{1,0:T(8,128)S(1)}, s32[64]{0:T(128)S(1)}) custom-call(s32[1,64]{1,0:T(1,128)S(1)} %copy-done.6, f32[2048,256]{1,0:T(8,128)S(1)} %copy-done), custom_call_target="tpu_custom_call" | custom-call | tf_op jit(solution)/shard_map/prep/pallas_call | solution.py:67
  5.7 0.0 copy-done.1
  5.7 0.0 copy-done.2
  5.7 0.0 copy-done.3
  5.7 0.0 copy-done.4
  5.8 0.0 copy-done.5
  5.8 59.8 %main.1 = (f32[512,256]{1,0:T(8,128)S(1)}, f32[1,512]{1,0:T(1,128)S(1)}) custom-call(s32[1,1,4]{2,1,0:T(1,128)S(1)} %copy-done.5, s32[64]{0:T(128)S(1)} %get-tuple-element.9.order_ref, bf16[1,1,1024,256]{3,2,1,0:T(8,128)(2,1)S(1)} %copy-done.1, bf16[256,1024]{1,0:T(8,128)(2,1)S(1)} %copy-done.2, bf16[256,256]{1,0:T(8,128)(2,1)S(1)} %copy-done.3, ...), custom_call_target="tpu_custom_call" | custom-call | tf_op jit(solution)/shard_map/main/pallas_call | solution.py:330
  65.6 2.2 %finish.1 = (f32[2048,256]{1,0:T(8,128)}, f32[1,512]{1,0:T(1,128)}) custom-call(s32[64]{0:T(128)S(1)} %get-tuple-element.9.order_ref, f32[512,256]{1,0:T(8,128)S(1)} %get-tuple-element.11.grad_ref, f32[512,256]{1,0:T(8,128)S(1)} %get-tuple-element.12.raw_ref, f32[1,512]{1,0:T(1,128)S(1)} %get-tuple-element.13.loss_in), custom_call_target="tpu_custom_call" | custom-call | tf_op jit(solution)/shard_map/finish/pallas_call | solution.py:379
Async XLA Ops:
  0.6 1.6 %copy-start = (f32[2048,256]{1,0:T(8,128)S(1)}, f32[2048,256]{1,0:T(8,128)}, u32[]{:S(2)}) copy-start(f32[2048,256]{1,0:T(8,128)} %table_ref.1) | copy-start | bytes 6291460
  2.2 0.7 copy-start.6
  2.9 2.8 %copy-start.1 = (bf16[1,1,1024,256]{3,2,1,0:T(8,128)(2,1)S(1)}, bf16[1,1,1024,256]{3,2,1,0:T(8,128)(2,1)}, u32[]{:S(2)}) copy-start(bf16[1,1,1024,256]{3,2,1,0:T(8,128)(2,1)} %hist_ref.1) | copy-start | bytes 1572868
  2.9 2.8 %copy-start.2 = (bf16[256,1024]{1,0:T(8,128)(2,1)S(1)}, bf16[256,1024]{1,0:T(8,128)(2,1)}, u32[]{:S(2)}) copy-start(bf16[256,1024]{1,0:T(8,128)(2,1)} %win_ref.1) | copy-start | bytes 1572868
  2.9 2.9 %copy-start.3 = (bf16[256,256]{1,0:T(8,128)(2,1)S(1)}, bf16[256,256]{1,0:T(8,128)(2,1)}, u32[]{:S(2)}) copy-start(bf16[256,256]{1,0:T(8,128)(2,1)} %wout_ref.1) | copy-start | bytes 393220
  2.9 2.9 %copy-start.4 = (s32[1,16,512]{2,1,0:T(8,128)S(1)}, s32[1,16,512]{2,1,0:T(8,128)}, u32[]{:S(2)}) copy-start(s32[1,16,512]{2,1,0:T(8,128)} %targets_ref.1) | copy-start | bytes 98308
  2.9 2.9 %copy-start.5 = (s32[1,1,4]{2,1,0:T(1,128)S(1)}, s32[1,1,4]{2,1,0:T(1,128)}, u32[]{:S(2)}) copy-start(s32[1,1,4]{2,1,0:T(1,128)} %len_ref.1) | copy-start | bytes 52

commit v2 on v1

v2 whole, which is shorter than its diff:
```python
import math

import jax
import jax.numpy as jnp
from jax import lax
from jax.experimental import pallas as pl
from jax.experimental.pallas import tpu as pltpu
from jax.sharding import PartitionSpec as P

D = 256
DH = 128
BLOCK = 128
GROUP = 16
SIDE = 4
SLOTS = 1024
TILE = 256
TILES = SLOTS // TILE
PART = TILE // GROUP
PAIR = SLOTS // GROUP
TOK = 512
CAND = 512
SCALE = 20.0
EARLY = 2
ARRIVE = (1, 3, 2)
HALF = TOK // 2
FAR_FIRST = (8, 9, 7, 10, 6, 11, 5, 12, 4, 13, 3, 14, 2, 15, 1)
MESH = pl.DeviceIdType.MESH
F32 = jnp.float32
BF16 = jnp.bfloat16


def unit_scale(rows):
    return lax.rsqrt(jnp.mean(rows * rows, axis=-1, keepdims=True) + 1e-06)


def silu(x):
    half = 0.5 * x
    return half + half * jnp.tanh(half)


def main_kernel(
    len_ref,
    neg_ref,
    hist_ref,
    win_ref,
    wout_ref,
    table_ref,
    targets_ref,
    grad_ref,
    loss_ref,
    own_ref,
    proj,
    enc,
    tot,
    units,
    send,
    recv,
    tok,
    cand,
    expd,
    sums,
    gsend,
    grecv,
    hits,
    raw_ref,
    tot_s,
    tot_r,
    a2a_s,
    a2a_r,
    cand_s,
    cand_r,
    tok_s,
    tok_r,
    sum_s,
    sum_r,
    hit_s,
    hit_r,
    g_s,
    g_r,
):
    me = lax.axis_index("wide")
    narrow = lax.axis_index("narrow")
    core = lax.rem(me, 2)
    tok_step = 4 - 3 * core
    cand_step = 1 + 3 * core
    my_t = lax.rem(narrow // tok_step, SIDE)
    my_c = lax.rem(narrow // cand_step, SIDE)

    def wide_peer(d):
        return (lax.rem(me + d, GROUP), narrow)

    def tok_peer(s):
        return (me, lax.rem(my_t + s, SIDE) * tok_step + my_c * cand_step)

    def cand_peer(s):
        return (me, my_t * tok_step + lax.rem(my_c + s, SIDE) * cand_step)

    def remote(src, dst, ssem, rsem, peer):
        return pltpu.make_async_remote_copy(
            src_ref=src, dst_ref=dst, send_sem=ssem, recv_sem=rsem, device_id=peer, device_id_type=MESH
        )

    barrier = pltpu.get_barrier_semaphore()
    for d in FAR_FIRST:
        pl.semaphore_signal(barrier, inc=1, device_id=wide_peer(d), device_id_type=MESH)
    for s in range(1, SIDE):
        pl.semaphore_signal(barrier, inc=1, device_id=tok_peer(s), device_id_type=MESH)
        pl.semaphore_signal(barrier, inc=1, device_id=cand_peer(s), device_id_type=MESH)

    e0 = len_ref[0, 0, 0]
    e1 = e0 + len_ref[0, 0, 1]
    e2 = e1 + len_ref[0, 0, 2]
    e3 = e2 + len_ref[0, 0, 3]
    tot[me] = jnp.full((8, 128), e3, jnp.int32)

    for b in range(TILES):
        rows = pl.ds(b * TILE, TILE)
        x = jnp.dot(hist_ref[0, 0, rows, :], win_ref[...], preferred_element_type=F32)
        proj[rows, :] = silu(x).astype(BF16)

    my_dev = me * GROUP + narrow
    blocks = [neg_ref[narrow * 4 + q] for q in range(4)]
    row8 = lax.broadcasted_iota(jnp.int32, (8, TOK), 0)
    row8s = row8[:, :128]
    held = jnp.zeros((8, 128), jnp.int32)
    for q in range(4):
        held = jnp.where(row8s == q, blocks[q], held)
    own_ref[...] = held * BLOCK
    own = [jnp.full((16, D), blocks[q] - my_dev * 16, jnp.int32) for q in range(4)]

    @pl.loop(0, BLOCK // 16)
    def _(i):
        at = pl.multiple_of(i * 16, 16)
        picked = [jnp.zeros((16, D), F32)] * 4
        for b in range(16):
            rows = table_ref[pl.ds(b * BLOCK + at, 16), :]
            picked = [jnp.where(own[q] == b, rows, picked[q]) for q in range(4)]
        for q in range(4):
            raw_ref[pl.ds(q * BLOCK + at, 16), :] = picked[q]

    rows = raw_ref[...]
    units[...] = (rows * unit_scale(rows) * 0.0625).astype(BF16)
    cand[my_c] = units[...]

    lanes = lax.broadcasted_iota(jnp.int32, (TILE, TILE), 1)
    subs = lax.broadcasted_iota(jnp.int32, (TILE, TILE), 0)

    def encode(b):
        rows = pl.ds(b * TILE, TILE)
        place = subs + b * TILE
        start = jnp.maximum(
            jnp.maximum(jnp.where(place >= e0, e0, 0), jnp.where(place >= e1, e1, 0)),
            jnp.maximum(jnp.where(place >= e2, e2, 0), jnp.where(place >= e3, e3, 0)),
        )
        share = 1.0 / (place - start + 1).astype(F32)
        heads = []
        for h in range(2):
            q = proj[rows, pl.ds(512 + h * DH, DH)]
            total = jnp.zeros((TILE, DH), F32)
            for kb in range(b + 1):
                krows = pl.ds(kb * TILE, TILE)
                k = proj[krows, pl.ds(768 + h * DH, DH)]
                v = proj[krows, pl.ds(256 + h * DH, DH)]
                scores = lax.dot_general(q, k, (((1,), (1,)), ((), ())), preferred_element_type=F32)
                weights = silu(scores * (DH ** -0.5)) * share
                allowed = lanes + kb * TILE >= start
                if kb == b:
                    allowed = allowed & (lanes <= subs)
                weights = jnp.where(allowed, weights, 0.0).astype(BF16)
                total = total + jnp.dot(weights, v, preferred_element_type=F32)
            heads.append(total)
        attended = jnp.concatenate(heads, axis=1)
        centred = attended - jnp.mean(attended, axis=-1, keepdims=True)
        spread = jnp.mean(centred * centred, axis=-1, keepdims=True)
        gate = proj[rows, pl.ds(0, D)].astype(F32)
        mixed = (centred * lax.rsqrt(spread + 1e-05) * gate).astype(BF16)
        state = hist_ref[0, 0, rows, :].astype(F32) + jnp.dot(mixed, wout_ref[...], preferred_element_type=F32)
        enc[rows, :] = jnp.where(place < e3, state * unit_scale(state) * 0.0625, 0.0).astype(BF16)

    for b in range(EARLY):
        encode(b)

    pl.semaphore_wait(barrier, GROUP - 1 + 2 * (SIDE - 1))
    tot_copies = [remote(tot.at[me], tot.at[me], tot_s.at[d], tot_r.at[d], wide_peer(d)) for d in FAR_FIRST]
    cand_copies = [
        remote(units, cand.at[my_c], cand_s.at[s], cand_r.at[s], cand_peer(s)) for s in range(1, SIDE)
    ]
    for copy in tot_copies + cand_copies:
        copy.start()

    for b in range(EARLY, TILES):
        encode(b)

    for copy in tot_copies:
        copy.wait_recv()
    begin = jnp.zeros((8, 128), jnp.int32)
    for w in range(GROUP):
        begin = begin + jnp.where(w < me, tot[w], 0)
    begin = jnp.concatenate([begin[0:1, :]] * 2, axis=1)
    wanted = (subs & 15) * 16 + (((subs >> 4) - begin) & 15)
    take = (lanes == wanted).astype(F32).astype(BF16)
    for b in range(TILES):
        packed = jnp.dot(take, enc[pl.ds(b * TILE, TILE), :], preferred_element_type=F32).astype(BF16)
        send[b] = packed.reshape(GROUP, PART, D)
        for d in FAR_FIRST:
            dest = lax.rem(me + d, GROUP)
            remote(
                send.at[b, dest], recv.at[me, pl.ds(b * PART, PART)], a2a_s, a2a_r, wide_peer(d)
            ).start()
        recv[me, pl.ds(b * PART, PART), :] = send[b, me]

    lane = lax.broadcasted_iota(jnp.int32, (1, 128), 1)
    slot = lax.broadcasted_iota(jnp.int32, (TOK, 128), 0)
    begin = jnp.zeros((1, 128), jnp.int32)
    pieces = []
    for w in range(0, GROUP, 2):
        second = begin + tot[w, 0:1, :]
        base = jnp.where(lane < PAIR, begin, second)
        goes_to = ((base - me + 15) >> 4) + (lane & (PAIR - 1))
        pieces.append((slot == goes_to).astype(F32).astype(BF16))
        begin = second + tot[w + 1, 0:1, :]
    gather = jnp.concatenate(pieces, axis=1)
    pltpu.make_async_copy(recv.at[pl.ds(0, GROUP - 1)], recv.at[pl.ds(0, GROUP - 1)], a2a_r).wait()
    own_tok = jnp.dot(gather, recv[...].reshape(GROUP * PAIR, D), preferred_element_type=F32).astype(BF16)
    tok[my_t] = own_tok

    tok_copies = {
        s: remote(tok.at[my_t], tok.at[my_t], tok_s.at[s], tok_r.at[s], tok_peer(s)) for s in ARRIVE
    }
    for key in ARRIVE:
        tok_copies[key].start()
    for copy in cand_copies:
        copy.wait_recv()

    part = jnp.zeros((8, TOK), F32)
    for s in (0,) + ARRIVE:
        if s:
            tok_copies[s].wait_recv()
        t = lax.rem(my_t + SIDE - s, SIDE)

        def forward(c, total):
            scores = lax.dot_general(
                cand[c], tok[t], (((1,), (1,)), ((), ())), preferred_element_type=F32
            )
            value = jnp.exp2(scores * (SCALE * math.log2(math.e)))
            expd[t, pl.ds(pl.multiple_of(c * CAND, CAND), CAND), :] = value
            return total + jnp.sum(value.reshape(CAND // 8, 8, TOK), axis=0)

        total = lax.fori_loop(0, SIDE, forward, jnp.zeros((8, TOK), F32))
        part = jnp.where(row8 == t, jnp.sum(total, axis=0, keepdims=True), part)
    sums[my_t] = part
    sum_copies = [
        remote(sums.at[my_t], sums.at[my_t], sum_s.at[s], sum_r.at[s], tok_peer(s)) for s in range(1, SIDE)
    ]
    for s in (2, 1, 3):
        sum_copies[s - 1].start()

    offset = lax.broadcasted_iota(jnp.int32, (BLOCK, TOK), 0)

    def block_start(c, q):
        return neg_ref[(my_t * tok_step + c * cand_step) * 4 + q] * BLOCK

    def target_of(t):
        return targets_ref[0, pl.ds(t * tok_step + my_c * cand_step, 1), :]

    for copy in sum_copies:
        copy.wait_recv()
    sumexp = (sums[0] + sums[1]) + (sums[2] + sums[3])
    inverse = 1.0 / sumexp

    g_copies = []
    part = jnp.zeros((8, TOK), F32)
    for s in (2, 1, 3, 0):
        c = lax.rem(my_c + s, SIDE)
        for half in range(2):
            total = jnp.zeros((2 * BLOCK, D), F32)
            for t in range(SIDE):
                target = target_of(t)
                scale_t = inverse[t : t + 1, :]
                slopes = []
                found = jnp.zeros((8, TOK), F32)
                for q in (2 * half, 2 * half + 1):
                    value = expd[t, pl.ds(pl.multiple_of(c * CAND + q * BLOCK, BLOCK), BLOCK), :]
                    hit = offset == target - block_start(c, q)
                    slopes.append((value * scale_t - jnp.where(hit, 1.0, 0.0)).astype(BF16))
                    found = found + jnp.sum(jnp.where(hit, value, 0.0).reshape(BLOCK // 8, 8, TOK), axis=0)
                total = total + jnp.dot(jnp.concatenate(slopes, axis=0), tok[t], preferred_element_type=F32)
                part = part + jnp.where(row8 == t, jnp.sum(found, axis=0, keepdims=True), 0.0)
            rows = pl.ds(half * 2 * BLOCK, 2 * BLOCK)
            if s:
                gsend[s, rows, :] = (SCALE * total).astype(BF16)
            else:
                grad_ref[rows, :] = SCALE * total
        if s:
            copy = remote(gsend.at[s], grecv.at[s], g_s.at[s], g_r.at[s], cand_peer(s))
            copy.start()
            g_copies.append(copy)
    hits[my_t] = part
    hit_copies = [
        remote(hits.at[my_t], hits.at[my_t], hit_s.at[s], hit_r.at[s], tok_peer(s)) for s in range(1, SIDE)
    ]
    for s in (2, 1, 3):
        hit_copies[s - 1].start()
    for copy in hit_copies:
        copy.wait_recv()
    found = (hits[0] + hits[1]) + (hits[2] + hits[3])
    loss = jnp.where(row8 == my_t, jnp.log(sumexp) - jnp.log(found), 0.0)
    loss_ref[...] = jnp.sum(loss, axis=0, keepdims=True)
    for copy in g_copies:
        copy.wait_recv()
    for q in range(4):
        at = pl.ds(q * BLOCK, BLOCK)
        grad = (grad_ref[at, :] + grecv[1, at, :].astype(F32)) + (
            grecv[2, at, :].astype(F32) + grecv[3, at, :].astype(F32)
        )
        rows = raw_ref[at, :]
        scale = unit_scale(rows)
        along = jnp.mean(rows * grad, axis=-1, keepdims=True)
        grad_ref[at, :] = (grad - rows * (scale * scale * along)) * (scale * 0.0625)

    for copy in tot_copies + cand_copies + list(tok_copies.values()) + sum_copies + hit_copies + g_copies:
        copy.wait_send()
    pltpu.make_async_copy(recv.at[pl.ds(0, GROUP - 1)], recv.at[pl.ds(0, GROUP - 1)], a2a_s).wait()


def main(lengths, neg_blocks, histories, w_in, w_out, item_table, targets):
    dma = pltpu.SemaphoreType.DMA
    anywhere = pl.BlockSpec(memory_space=pl.ANY)
    vmem = pl.BlockSpec(memory_space=pltpu.VMEM)
    smem = pl.BlockSpec(memory_space=pltpu.SMEM)
    return pl.pallas_call(
        main_kernel,
        out_shape=(
            jax.ShapeDtypeStruct((CAND, D), F32),
            jax.ShapeDtypeStruct((1, TOK), F32),
            jax.ShapeDtypeStruct((8, 128), jnp.int32),
        ),
        in_specs=[smem, smem, vmem, vmem, vmem, vmem, vmem],
        out_specs=(vmem, vmem, vmem),
        scratch_shapes=[
            pltpu.VMEM((SLOTS, 4 * D), BF16),
            pltpu.VMEM((SLOTS, D), BF16),
            pltpu.VMEM((GROUP, 8, 128), jnp.int32),
            pltpu.VMEM((CAND, D), BF16),
            pltpu.VMEM((TILES, GROUP, PART, D), BF16),
            pltpu.VMEM((GROUP, PAIR, D), BF16),
            pltpu.VMEM((SIDE, TOK, D), BF16),
            pltpu.VMEM((SIDE, CAND, D), BF16),
            pltpu.VMEM((SIDE, SIDE * CAND, TOK), F32),
            pltpu.VMEM((SIDE, 8, TOK), F32),
            pltpu.VMEM((SIDE, CAND, D), BF16),
            pltpu.VMEM((SIDE, CAND, D), BF16),
            pltpu.VMEM((SIDE, 8, TOK), F32),
            pltpu.VMEM((CAND, D), F32),
            dma((GROUP,)),
            dma((GROUP,)),
            dma,
            dma,
        ]
        + [dma((SIDE,))] * 2
        + [dma((2 * SIDE,))] * 2
        + [dma((SIDE,))] * 4
        + [dma((2 * SIDE,))] * 2,
        compiler_params=pltpu.CompilerParams(
            collective_id=0, has_side_effects=True, vmem_limit_bytes=56 * 2**20
        ),
        name="main",
    )(lengths, neg_blocks, histories, w_in, w_out, item_table, targets)


def finish_kernel(own_hbm, value_hbm, loss_in, out_hbm, loss_hbm, zeros, value_ref, loss_ref, own_ref, in_s, out_s):
    first = (lax.axis_index("wide") * GROUP + lax.axis_index("narrow")) * 16 * BLOCK
    loads = [
        pltpu.make_async_copy(own_hbm, own_ref, in_s.at[0]),
        pltpu.make_async_copy(loss_in, loss_ref, in_s.at[1]),
        pltpu.make_async_copy(value_hbm, value_ref, in_s.at[2]),
    ]
    for load in loads:
        load.start()
    zeros[...] = jnp.zeros_like(zeros)
    blanks = [
        pltpu.make_async_copy(zeros, out_hbm.at[pl.ds(i * CAND, CAND)], out_s.at[i]) for i in range(4)
    ]
    for blank in blanks:
        blank.start()
    loads[1].wait()
    moves = [pltpu.make_async_copy(loss_ref, loss_hbm, out_s.at[8])]
    moves[0].start()
    loads[0].wait()
    loads[2].wait()
    for blank in blanks:
        blank.wait()
    for q in range(4):
        at = pl.multiple_of(own_ref[q, 0] - first, BLOCK)
        moves.append(
            pltpu.make_async_copy(
                value_ref.at[pl.ds(q * BLOCK, BLOCK)], out_hbm.at[pl.ds(at, BLOCK)], out_s.at[4 + q]
            )
        )
        moves[-1].start()
    for move in moves:
        move.wait()


def finish(own, value, loss):
    anywhere = pl.BlockSpec(memory_space=pl.ANY)
    return pl.pallas_call(
        finish_kernel,
        out_shape=(jax.ShapeDtypeStruct((16 * BLOCK, D), F32), jax.ShapeDtypeStruct((1, TOK), F32)),
        in_specs=[anywhere] * 3,
        out_specs=(anywhere, anywhere),
        scratch_shapes=[
            pltpu.VMEM((CAND, D), F32),
            pltpu.VMEM((CAND, D), F32),
            pltpu.VMEM((1, TOK), F32),
            pltpu.SMEM((8, 128), jnp.int32),
            pltpu.SemaphoreType.DMA((3,)),
            pltpu.SemaphoreType.DMA((9,)),
        ],
        compiler_params=pltpu.CompilerParams(vmem_limit_bytes=56 * 2**20),
        name="finish",
    )(own, value, loss)


def local(histories, lengths, w_in, w_out, item_table, neg_blocks, targets):
    blocks = neg_blocks[0]
    rank = jnp.sum((blocks[None, :] < blocks[:, None]).astype(jnp.int32), axis=1)
    places = jnp.arange(blocks.shape[0], dtype=jnp.int32)
    order = jnp.sum(jnp.where(rank[:, None] == places[None, :], blocks[:, None], 0), axis=0)
    value, loss, own = main(lengths, order, histories, w_in, w_out, item_table, targets)
    item_grad, loss = finish(own, value, loss)
    return (loss[None], item_grad)


def solution(mesh):
    in_specs = (
        P("wide", "narrow", None, None),
        P("wide", "narrow", None),
        P(),
        P(),
        P(("wide", "narrow"), None),
        P("wide", None),
        P("wide", None, None),
    )
    out_specs = (P("wide", "narrow", None), P(("wide", "narrow"), None))
    return jax.shard_map(local, mesh=mesh, in_specs=in_specs, out_specs=out_specs, check_vma=False)
```

time: 68.2 us -> 62.1 us (0.911)
  Pallas kernels: 64.8 us -> 58.7 us
  local copies, waits for them, and re-layouts: 2.26 us -> 0 us
  other arithmetic: 0 us -> 2.18 us
    pallas_call x1, Pallas kernels: 59.8 us -> 56.4 us  [main(): pl.pallas_call(main_kernel, out_shape=(jax.ShapeDtypeStruct((CAND, D), F3...]
    pallas_call x1 -> x0, Pallas kernels: 2.8 us -> none  [prep(): pl.pallas_call(prep_kernel, out_shape=(jax.ShapeDtypeStruct((CAND, D), BF...]
    unnamed x14 -> x0, local copies, waits for them, and re-layouts: 2.26 us -> none
    reduce_sum x0 -> x2, other arithmetic: none -> 2.18 us  [the longest x1 1.27 us: local(): jnp.sum(jnp.where(rank[:, None] == places[None, :], blocks[:, None], 0),...]
where the time goes in v2:
time: 62.1 us; the launch traced here: 61.5 us
  Pallas kernels  58.7 us (95%)
  other arithmetic  2.18 us (4%)
  between operations  0.64 us (1%)
    pallas_call x1, Pallas kernels, main(): pl.pallas_call(main_kernel, out_shape=(jax.ShapeDtypeStruct((CAND, D), F3...  56.4 us
    pallas_call x1, Pallas kernels, finish(): pl.pallas_call(finish_kernel, out_shape=(jax.ShapeDtypeStruct((16 * BLOCK...  2.23 us
    reduce_sum x1, other arithmetic, local(): jnp.sum(jnp.where(rank[:, None] == places[None, :], blocks[:, None], 0),...  1.27 us

profile of v2, /device:TPU:2, one launch (start us, length us, event | category | flops | bytes accessed | tf_op | source)
XLA Modules:
  0.0 61.5 jit_solution(18212270059831853882)
XLA Ops:
  0.6 0.9 %convert_reduce_fusion = s32[64]{0:T(128)S(1)} fusion(s32[64]{0:T(128)} %bitcast.3), kind=kLoop, calls=%fused_computation.2 | loop fusion | flops 12224 | bytes 512 | tf_op jit(solution)/shard_map/reduce_sum | solution.py:427
  1.5 1.3 %select_reduce_fusion.neg_ref = s32[64]{0:T(128)} fusion(s32[64]{0:T(128)S(1)} %convert_reduce_fusion, s32[64]{0:T(128)} %bitcast.4), kind=kLoop, calls=%fused_computation | loop fusion | flops 12224 | bytes 768 | tf_op jit(solution)/shard_map/reduce_sum | solution.py:429
  2.8 56.4 %main.1 = (f32[512,256]{1,0:T(8,128)}, f32[1,512]{1,0:T(1,128)}, s32[8,128]{1,0:T(8,128)}) custom-call(s32[1,1,4]{2,1,0:T(1,128)} %len_ref.1, s32[64]{0:T(128)} %select_reduce_fusion.neg_ref, bf16[1,1,1024,256]{3,2,1,0:T(8,128)(2,1)} %hist_ref.1, bf16[256,1024]{1,0:T(8,128)(2,1)} %win_ref.1, bf16[256,256]{1,0:T(8,128)(2,1)} %wout_ref.1, ...), custom_call_target="tpu_custom_call" | custom-call | tf_op jit(solution)/shard_map/main/pallas_call | solution.py:331
  59.3 2.2 %finish.1 = (f32[2048,256]{1,0:T(8,128)}, f32[1,512]{1,0:T(1,128)}) custom-call(s32[8,128]{1,0:T(8,128)} %get-tuple-element.7.own_hbm, f32[512,256]{1,0:T(8,128)} %get-tuple-element.8.value_hbm, f32[1,512]{1,0:T(1,128)} %get-tuple-element.9.loss_in), custom_call_target="tpu_custom_call" | custom-call | tf_op jit(solution)/shard_map/finish/pallas_call | solution.py:407

commit v3 on v2

--- a/solution.py
+++ b/solution.py
@@ -21,9 +21,10 @@
 CAND = 512
 SCALE = 20.0
 EARLY = 2
-ARRIVE = (1, 3, 2)
+ARRIVE = ((1, 0), (3, 0), (1, 1), (3, 1), (2, 0), (2, 1))
 HALF = TOK // 2
 FAR_FIRST = (8, 9, 7, 10, 6, 11, 5, 12, 4, 13, 3, 14, 2, 15, 1)
+NEAR_FIRST = FAR_FIRST[::-1]
 MESH = pl.DeviceIdType.MESH
 F32 = jnp.float32
 BF16 = jnp.bfloat16
@@ -39,6 +40,16 @@
 
 
 def main_kernel(
+    len_hbm,
+    neg_hbm,
+    hist_hbm,
+    win_hbm,
+    wout_hbm,
+    table_hbm,
+    targets_hbm,
+    value_hbm,
+    loss_hbm,
+    own_hbm,
     len_ref,
     neg_ref,
     hist_ref,
@@ -46,12 +57,10 @@
     wout_ref,
     table_ref,
     targets_ref,
-    grad_ref,
-    loss_ref,
-    own_ref,
     proj,
     enc,
     tot,
+    own_ref,
     units,
     send,
     recv,
@@ -62,7 +71,12 @@
     gsend,
     grecv,
     hits,
+    grad_ref,
     raw_ref,
+    begin_ref,
+    loss_ref,
+    out_s,
+    in_s,
     tot_s,
     tot_r,
     a2a_s,
@@ -107,25 +121,49 @@
         pl.semaphore_signal(barrier, inc=1, device_id=tok_peer(s), device_id_type=MESH)
         pl.semaphore_signal(barrier, inc=1, device_id=cand_peer(s), device_id_type=MESH)
 
+    loads = [
+        pltpu.make_async_copy(src, dst, in_s.at[i])
+        for i, (src, dst) in enumerate(
+            [
+                (len_hbm, len_ref),
+                (neg_hbm, neg_ref),
+                (hist_hbm, hist_ref),
+                (win_hbm, win_ref),
+                (wout_hbm, wout_ref),
+                (table_hbm, table_ref),
+                (targets_hbm, targets_ref),
+            ]
+        )
+    ]
+    for load in loads:
+        load.start()
+    load_len, load_neg, load_hist, load_win, load_wout, load_table, load_targets = loads
+
+    load_len.wait()
     e0 = len_ref[0, 0, 0]
     e1 = e0 + len_ref[0, 0, 1]
     e2 = e1 + len_ref[0, 0, 2]
     e3 = e2 + len_ref[0, 0, 3]
     tot[me] = jnp.full((8, 128), e3, jnp.int32)
 
+    load_hist.wait()
+    load_win.wait()
     for b in range(TILES):
         rows = pl.ds(b * TILE, TILE)
         x = jnp.dot(hist_ref[0, 0, rows, :], win_ref[...], preferred_element_type=F32)
         proj[rows, :] = silu(x).astype(BF16)
 
+    load_neg.wait()
     my_dev = me * GROUP + narrow
     blocks = [neg_ref[narrow * 4 + q] for q in range(4)]
     row8 = lax.broadcasted_iota(jnp.int32, (8, TOK), 0)
     row8s = row8[:, :128]
+    half_of = lax.broadcasted_iota(jnp.int32, (8, TOK), 1) >> 8
     held = jnp.zeros((8, 128), jnp.int32)
     for q in range(4):
         held = jnp.where(row8s == q, blocks[q], held)
     own_ref[...] = held * BLOCK
+    load_table.wait()
     own = [jnp.full((16, D), blocks[q] - my_dev * 16, jnp.int32) for q in range(4)]
 
     @pl.loop(0, BLOCK // 16)
@@ -144,6 +182,7 @@
 
     lanes = lax.broadcasted_iota(jnp.int32, (TILE, TILE), 1)
     subs = lax.broadcasted_iota(jnp.int32, (TILE, TILE), 0)
+    load_wout.wait()
 
     def encode(b):
         rows = pl.ds(b * TILE, TILE)
@@ -191,24 +230,35 @@
     for b in range(EARLY, TILES):
         encode(b)
 
-    for copy in tot_copies:
-        copy.wait_recv()
-    begin = jnp.zeros((8, 128), jnp.int32)
-    for w in range(GROUP):
-        begin = begin + jnp.where(w < me, tot[w], 0)
+    low = me < GROUP // 2
+    begin_ref[...] = jnp.where(low, 0, -e3) + jnp.zeros((8, 128), jnp.int32)
+
+    def near(d):
+        w = lax.rem(me + GROUP - d, GROUP)
+        return (low & (w < me)) | (jnp.logical_not(low) & (w > me))
+
+    for d, copy in zip(NEAR_FIRST, tot_copies[::-1]):
+
+        @pl.when(near(d))
+        def _():
+            copy.wait_recv()
+            other = tot[lax.rem(me + GROUP - d, GROUP)]
+            begin_ref[...] += jnp.where(low, other, -other)
+
+    begin = begin_ref[...]
     begin = jnp.concatenate([begin[0:1, :]] * 2, axis=1)
     wanted = (subs & 15) * 16 + (((subs >> 4) - begin) & 15)
     take = (lanes == wanted).astype(F32).astype(BF16)
     for b in range(TILES):
         packed = jnp.dot(take, enc[pl.ds(b * TILE, TILE), :], preferred_element_type=F32).astype(BF16)
-        send[b] = packed.reshape(GROUP, PART, D)
-        for d in FAR_FIRST:
-            dest = lax.rem(me + d, GROUP)
-            remote(
-                send.at[b, dest], recv.at[me, pl.ds(b * PART, PART)], a2a_s, a2a_r, wide_peer(d)
-            ).start()
-        recv[me, pl.ds(b * PART, PART), :] = send[b, me]
-
+        send[:, pl.ds(b * PART, PART), :] = packed.reshape(GROUP, PART, D)
+    for d in FAR_FIRST:
+        dest = lax.rem(me + d, GROUP)
+        remote(send.at[dest], recv.at[me], a2a_s, a2a_r, wide_peer(d)).start()
+    recv[me] = send[me]
+
+    for d, copy in zip(NEAR_FIRST, tot_copies[::-1]):
+        pl.when(jnp.logical_not(near(d)))(copy.wait_recv)
     lane = lax.broadcasted_iota(jnp.int32, (1, 128), 1)
     slot = lax.broadcasted_iota(jnp.int32, (TOK, 128), 0)
     begin = jnp.zeros((1, 128), jnp.int32)
@@ -222,10 +272,14 @@
     gather = jnp.concatenate(pieces, axis=1)
     pltpu.make_async_copy(recv.at[pl.ds(0, GROUP - 1)], recv.at[pl.ds(0, GROUP - 1)], a2a_r).wait()
     own_tok = jnp.dot(gather, recv[...].reshape(GROUP * PAIR, D), preferred_element_type=F32).astype(BF16)
-    tok[my_t] = own_tok
+    tok[2 * my_t] = own_tok[:HALF]
+    tok[2 * my_t + 1] = own_tok[HALF:]
 
     tok_copies = {
-        s: remote(tok.at[my_t], tok.at[my_t], tok_s.at[s], tok_r.at[s], tok_peer(s)) for s in ARRIVE
+        (s, h): remote(
+            tok.at[2 * my_t + h], tok.at[2 * my_t + h], tok_s.at[2 * s + h], tok_r.at[2 * s + h], tok_peer(s)
+        )
+        for s, h in ARRIVE
     }
     for key in ARRIVE:
         tok_copies[key].start()
@@ -233,21 +287,22 @@
         copy.wait_recv()
 
     part = jnp.zeros((8, TOK), F32)
-    for s in (0,) + ARRIVE:
+    for s, h in ((0, 0), (0, 1)) + ARRIVE:
         if s:
-            tok_copies[s].wait_recv()
+            tok_copies[s, h].wait_recv()
         t = lax.rem(my_t + SIDE - s, SIDE)
 
         def forward(c, total):
             scores = lax.dot_general(
-                cand[c], tok[t], (((1,), (1,)), ((), ())), preferred_element_type=F32
+                cand[c], tok[2 * t + h], (((1,), (1,)), ((), ())), preferred_element_type=F32
             )
             value = jnp.exp2(scores * (SCALE * math.log2(math.e)))
-            expd[t, pl.ds(pl.multiple_of(c * CAND, CAND), CAND), :] = value
-            return total + jnp.sum(value.reshape(CAND // 8, 8, TOK), axis=0)
-
-        total = lax.fori_loop(0, SIDE, forward, jnp.zeros((8, TOK), F32))
-        part = jnp.where(row8 == t, jnp.sum(total, axis=0, keepdims=True), part)
+            expd[t, pl.ds(pl.multiple_of(c * CAND, CAND), CAND), pl.ds(h * HALF, HALF)] = value
+            return total + jnp.sum(value.reshape(CAND // 8, 8, TOK // 2), axis=0)
+
+        total = lax.fori_loop(0, SIDE, forward, jnp.zeros((8, TOK // 2), F32))
+        total = jnp.concatenate([jnp.sum(total, axis=0, keepdims=True)] * 2, axis=1)
+        part = jnp.where((row8 == t) & (half_of == h), total, part)
     sums[my_t] = part
     sum_copies = [
         remote(sums.at[my_t], sums.at[my_t], sum_s.at[s], sum_r.at[s], tok_peer(s)) for s in range(1, SIDE)
@@ -255,6 +310,7 @@
     for s in (2, 1, 3):
         sum_copies[s - 1].start()
 
+    load_targets.wait()
     offset = lax.broadcasted_iota(jnp.int32, (BLOCK, TOK), 0)
 
     def block_start(c, q):
@@ -284,17 +340,22 @@
                     hit = offset == target - block_start(c, q)
                     slopes.append((value * scale_t - jnp.where(hit, 1.0, 0.0)).astype(BF16))
                     found = found + jnp.sum(jnp.where(hit, value, 0.0).reshape(BLOCK // 8, 8, TOK), axis=0)
-                total = total + jnp.dot(jnp.concatenate(slopes, axis=0), tok[t], preferred_element_type=F32)
+                total = total + jnp.dot(jnp.concatenate(slopes, axis=0), tok[2 * t : 2 * t + 2].reshape(TOK, D), preferred_element_type=F32)
                 part = part + jnp.where(row8 == t, jnp.sum(found, axis=0, keepdims=True), 0.0)
             rows = pl.ds(half * 2 * BLOCK, 2 * BLOCK)
             if s:
-                gsend[s, rows, :] = (SCALE * total).astype(BF16)
+                gsend[2 * s + half] = (SCALE * total).astype(BF16)
+                copy = remote(
+                    gsend.at[2 * s + half],
+                    grecv.at[2 * s + half],
+                    g_s.at[2 * s + half],
+                    g_r.at[2 * s + half],
+                    cand_peer(s),
+                )
+                copy.start()
+                g_copies.append(copy)
             else:
                 grad_ref[rows, :] = SCALE * total
-        if s:
-            copy = remote(gsend.at[s], grecv.at[s], g_s.at[s], g_r.at[s], cand_peer(s))
-            copy.start()
-            g_copies.append(copy)
     hits[my_t] = part
     hit_copies = [
         remote(hits.at[my_t], hits.at[my_t], hit_s.at[s], hit_r.at[s], tok_peer(s)) for s in range(1, SIDE)
@@ -306,28 +367,38 @@
     found = (hits[0] + hits[1]) + (hits[2] + hits[3])
     loss = jnp.where(row8 == my_t, jnp.log(sumexp) - jnp.log(found), 0.0)
     loss_ref[...] = jnp.sum(loss, axis=0, keepdims=True)
-    for copy in g_copies:
-        copy.wait_recv()
+    outs = [
+        pltpu.make_async_copy(loss_ref, loss_hbm, out_s.at[1]),
+        pltpu.make_async_copy(own_ref, own_hbm, out_s.at[2]),
+    ]
+    for copy in outs:
+        copy.start()
     for q in range(4):
+        if q % 2 == 0:
+            for s in range(3):
+                g_copies[2 * s + q // 2].wait_recv()
         at = pl.ds(q * BLOCK, BLOCK)
-        grad = (grad_ref[at, :] + grecv[1, at, :].astype(F32)) + (
-            grecv[2, at, :].astype(F32) + grecv[3, at, :].astype(F32)
+        part = pl.ds(q % 2 * BLOCK, BLOCK)
+        grad = (grad_ref[at, :] + grecv[2 + q // 2, part, :].astype(F32)) + (
+            grecv[4 + q // 2, part, :].astype(F32) + grecv[6 + q // 2, part, :].astype(F32)
         )
         rows = raw_ref[at, :]
         scale = unit_scale(rows)
         along = jnp.mean(rows * grad, axis=-1, keepdims=True)
         grad_ref[at, :] = (grad - rows * (scale * scale * along)) * (scale * 0.0625)
+    outs.append(pltpu.make_async_copy(grad_ref, value_hbm, out_s.at[0]))
+    outs[-1].start()
 
     for copy in tot_copies + cand_copies + list(tok_copies.values()) + sum_copies + hit_copies + g_copies:
         copy.wait_send()
+    for copy in outs:
+        copy.wait()
     pltpu.make_async_copy(recv.at[pl.ds(0, GROUP - 1)], recv.at[pl.ds(0, GROUP - 1)], a2a_s).wait()
 
 
 def main(lengths, neg_blocks, histories, w_in, w_out, item_table, targets):
     dma = pltpu.SemaphoreType.DMA
     anywhere = pl.BlockSpec(memory_space=pl.ANY)
-    vmem = pl.BlockSpec(memory_space=pltpu.VMEM)
-    smem = pl.BlockSpec(memory_space=pltpu.SMEM)
     return pl.pallas_call(
         main_kernel,
         out_shape=(
@@ -335,23 +406,36 @@
             jax.ShapeDtypeStruct((1, TOK), F32),
             jax.ShapeDtypeStruct((8, 128), jnp.int32),
         ),
-        in_specs=[smem, smem, vmem, vmem, vmem, vmem, vmem],
-        out_specs=(vmem, vmem, vmem),
+        in_specs=[anywhere] * 7,
+        out_specs=(anywhere, anywhere, anywhere),
         scratch_shapes=[
+            pltpu.SMEM((1, 1, 4), jnp.int32),
+            pltpu.SMEM((64,), jnp.int32),
+            pltpu.VMEM((1, 1, SLOTS, D), BF16),
+            pltpu.VMEM((D, 4 * D), BF16),
+            pltpu.VMEM((D, D), BF16),
+            pltpu.VMEM((16 * BLOCK, D), F32),
+            pltpu.VMEM((1, GROUP, TOK), jnp.int32),
             pltpu.VMEM((SLOTS, 4 * D), BF16),
             pltpu.VMEM((SLOTS, D), BF16),
             pltpu.VMEM((GROUP, 8, 128), jnp.int32),
+            pltpu.VMEM((8, 128), jnp.int32),
             pltpu.VMEM((CAND, D), BF16),
-            pltpu.VMEM((TILES, GROUP, PART, D), BF16),
             pltpu.VMEM((GROUP, PAIR, D), BF16),
-            pltpu.VMEM((SIDE, TOK, D), BF16),
+            pltpu.VMEM((GROUP, PAIR, D), BF16),
+            pltpu.VMEM((2 * SIDE, HALF, D), BF16),
             pltpu.VMEM((SIDE, CAND, D), BF16),
             pltpu.VMEM((SIDE, SIDE * CAND, TOK), F32),
             pltpu.VMEM((SIDE, 8, TOK), F32),
-            pltpu.VMEM((SIDE, CAND, D), BF16),
-            pltpu.VMEM((SIDE, CAND, D), BF16),
+            pltpu.VMEM((2 * SIDE, HALF, D), BF16),
+            pltpu.VMEM((2 * SIDE, HALF, D), BF16),
             pltpu.VMEM((SIDE, 8, TOK), F32),
             pltpu.VMEM((CAND, D), F32),
+            pltpu.VMEM((CAND, D), F32),
+            pltpu.VMEM((8, 128), jnp.int32),
+            pltpu.VMEM((1, TOK), F32),
+            dma((3,)),
+            dma((7,)),
             dma((GROUP,)),
             dma((GROUP,)),
             dma,

time: 62.1 us -> 61.7 us (level)
  no operation moved by 1% of the time
where the time goes in v3:
time: 61.7 us; the launch traced here: 61.5 us
  Pallas kernels  58.6 us (95%)
  other arithmetic  2.18 us (4%)
  between operations  0.8 us (1%)
    pallas_call x1, Pallas kernels, main(): pl.pallas_call(main_kernel, out_shape=(jax.ShapeDtypeStruct((CAND, D), F3...  56.3 us
    pallas_call x1, Pallas kernels, finish(): pl.pallas_call(finish_kernel, out_shape=(jax.ShapeDtypeStruct((16 * BLOCK...  2.23 us
    reduce_sum x1, other arithmetic, local(): jnp.sum(jnp.where(rank[:, None] == places[None, :], blocks[:, None], 0),...  1.27 us

profile of v3, /device:TPU:2, one launch (start us, length us, event | category | flops | bytes accessed | tf_op | source)
XLA Modules:
  0.0 61.5 jit_solution(14248953542856155502)
XLA Ops:
  0.6 0.9 %convert_reduce_fusion = s32[64]{0:T(128)S(1)} fusion(s32[64]{0:T(128)} %bitcast.3), kind=kLoop, calls=%fused_computation.2 | loop fusion | flops 12224 | bytes 512 | tf_op jit(solution)/shard_map/reduce_sum | solution.py:511
  1.5 1.3 %select_reduce_fusion.neg_hbm = s32[64]{0:T(128)} fusion(s32[64]{0:T(128)S(1)} %convert_reduce_fusion, s32[64]{0:T(128)} %bitcast.4), kind=kLoop, calls=%fused_computation | loop fusion | flops 12224 | bytes 768 | tf_op jit(solution)/shard_map/reduce_sum | solution.py:513
  2.8 56.3 %main.1 = (f32[512,256]{1,0:T(8,128)}, f32[1,512]{1,0:T(1,128)}, s32[8,128]{1,0:T(8,128)}) custom-call(s32[1,1,4]{2,1,0:T(1,128)} %len_hbm.1, s32[64]{0:T(128)} %select_reduce_fusion.neg_hbm, bf16[1,1,1024,256]{3,2,1,0:T(8,128)(2,1)} %hist_hbm.1, bf16[256,1024]{1,0:T(8,128)(2,1)} %win_hbm.1, bf16[256,256]{1,0:T(8,128)(2,1)} %wout_hbm.1, ...), custom_call_target="tpu_custom_call" | custom-call | tf_op jit(solution)/shard_map/main/pallas_call | solution.py:402
  59.1 2.2 %finish.1 = (f32[2048,256]{1,0:T(8,128)}, f32[1,512]{1,0:T(1,128)}) custom-call(s32[8,128]{1,0:T(8,128)} %get-tuple-element.7.own_hbm, f32[512,256]{1,0:T(8,128)} %get-tuple-element.8.value_hbm, f32[1,512]{1,0:T(1,128)} %get-tuple-element.9.loss_in), custom_call_target="tpu_custom_call" | custom-call | tf_op jit(solution)/shard_map/finish/pallas_call | solution.py:491

commit v4 on v3

--- a/solution.py
+++ b/solution.py
@@ -20,7 +20,7 @@
 TOK = 512
 CAND = 512
 SCALE = 20.0
-EARLY = 2
+EARLY = 1
 ARRIVE = ((1, 0), (3, 0), (1, 1), (3, 1), (2, 0), (2, 1))
 HALF = TOK // 2
 FAR_FIRST = (8, 9, 7, 10, 6, 11, 5, 12, 4, 13, 3, 14, 2, 15, 1)
@@ -153,33 +153,6 @@
         x = jnp.dot(hist_ref[0, 0, rows, :], win_ref[...], preferred_element_type=F32)
         proj[rows, :] = silu(x).astype(BF16)
 
-    load_neg.wait()
-    my_dev = me * GROUP + narrow
-    blocks = [neg_ref[narrow * 4 + q] for q in range(4)]
-    row8 = lax.broadcasted_iota(jnp.int32, (8, TOK), 0)
-    row8s = row8[:, :128]
-    half_of = lax.broadcasted_iota(jnp.int32, (8, TOK), 1) >> 8
-    held = jnp.zeros((8, 128), jnp.int32)
-    for q in range(4):
-        held = jnp.where(row8s == q, blocks[q], held)
-    own_ref[...] = held * BLOCK
-    load_table.wait()
-    own = [jnp.full((16, D), blocks[q] - my_dev * 16, jnp.int32) for q in range(4)]
-
-    @pl.loop(0, BLOCK // 16)
-    def _(i):
-        at = pl.multiple_of(i * 16, 16)
-        picked = [jnp.zeros((16, D), F32)] * 4
-        for b in range(16):
-            rows = table_ref[pl.ds(b * BLOCK + at, 16), :]
-            picked = [jnp.where(own[q] == b, rows, picked[q]) for q in range(4)]
-        for q in range(4):
-            raw_ref[pl.ds(q * BLOCK + at, 16), :] = picked[q]
-
-    rows = raw_ref[...]
-    units[...] = (rows * unit_scale(rows) * 0.0625).astype(BF16)
-    cand[my_c] = units[...]
-
     lanes = lax.broadcasted_iota(jnp.int32, (TILE, TILE), 1)
     subs = lax.broadcasted_iota(jnp.int32, (TILE, TILE), 0)
     load_wout.wait()
@@ -221,10 +194,49 @@
 
     pl.semaphore_wait(barrier, GROUP - 1 + 2 * (SIDE - 1))
     tot_copies = [remote(tot.at[me], tot.at[me], tot_s.at[d], tot_r.at[d], wide_peer(d)) for d in FAR_FIRST]
+    for copy in tot_copies:
+        copy.start()
+
+    load_neg.wait()
+    my_dev = me * GROUP + narrow
+    along = lax.broadcasted_iota(jnp.int32, (64, 64), 1)
+    down = lax.broadcasted_iota(jnp.int32, (64, 64), 0)
+    listed = jnp.broadcast_to(neg_ref[...].astype(F32), (64, 64))
+    column = jnp.sum(jnp.where(along == down, listed, 0.0), axis=1, keepdims=True)
+    rank = jnp.sum(jnp.where(listed < column, 1.0, 0.0), axis=1, keepdims=True)
+    ordered = jnp.sum(jnp.where(along.astype(F32) == rank, column, 0.0), axis=0, keepdims=True)
+
+    def block_at(k):
+        return jnp.sum(jnp.where(along[0:1, :] == k, ordered, 0.0), axis=1, keepdims=True).astype(jnp.int32)
+
+    blocks = [block_at(narrow * 4 + q) for q in range(4)]
+    row8 = lax.broadcasted_iota(jnp.int32, (8, TOK), 0)
+    row8s = row8[:, :128]
+    half_of = lax.broadcasted_iota(jnp.int32, (8, TOK), 1) >> 8
+    held = jnp.zeros((8, 128), jnp.int32)
+    for q in range(4):
+        held = jnp.where(row8s == q, blocks[q], held)
+    own_ref[...] = held * BLOCK
+    load_table.wait()
+    own = [jnp.broadcast_to(blocks[q] - my_dev * 16, (16, D)) for q in range(4)]
+
+    @pl.loop(0, BLOCK // 16)
+    def _(i):
+        at = pl.multiple_of(i * 16, 16)
+        picked = [jnp.zeros((16, D), F32)] * 4
+        for b in range(16):
+            rows = table_ref[pl.ds(b * BLOCK + at, 16), :]
+            picked = [jnp.where(own[q] == b, rows, picked[q]) for q in range(4)]
+        for q in range(4):
+            raw_ref[pl.ds(q * BLOCK + at, 16), :] = picked[q]
+
+    rows = raw_ref[...]
+    units[...] = (rows * unit_scale(rows) * 0.0625).astype(BF16)
+    cand[my_c] = units[...]
     cand_copies = [
         remote(units, cand.at[my_c], cand_s.at[s], cand_r.at[s], cand_peer(s)) for s in range(1, SIDE)
     ]
-    for copy in tot_copies + cand_copies:
+    for copy in cand_copies:
         copy.start()
 
     for b in range(EARLY, TILES):
@@ -313,8 +325,11 @@
     load_targets.wait()
     offset = lax.broadcasted_iota(jnp.int32, (BLOCK, TOK), 0)
 
-    def block_start(c, q):
-        return neg_ref[(my_t * tok_step + c * cand_step) * 4 + q] * BLOCK
+    starts = {}
+    for s in range(SIDE):
+        owner = my_t * tok_step + lax.rem(my_c + s, SIDE) * cand_step
+        for q in range(4):
+            starts[s, q] = block_at(owner * 4 + q) * BLOCK
 
     def target_of(t):
         return targets_ref[0, pl.ds(t * tok_step + my_c * cand_step, 1), :]
@@ -337,7 +352,7 @@
                 found = jnp.zeros((8, TOK), F32)
                 for q in (2 * half, 2 * half + 1):
                     value = expd[t, pl.ds(pl.multiple_of(c * CAND + q * BLOCK, BLOCK), BLOCK), :]
-                    hit = offset == target - block_start(c, q)
+                    hit = offset == target - starts[s, q]
                     slopes.append((value * scale_t - jnp.where(hit, 1.0, 0.0)).astype(BF16))
                     found = found + jnp.sum(jnp.where(hit, value, 0.0).reshape(BLOCK // 8, 8, TOK), axis=0)
                 total = total + jnp.dot(jnp.concatenate(slopes, axis=0), tok[2 * t : 2 * t + 2].reshape(TOK, D), preferred_element_type=F32)
@@ -410,7 +425,7 @@
         out_specs=(anywhere, anywhere, anywhere),
         scratch_shapes=[
             pltpu.SMEM((1, 1, 4), jnp.int32),
-            pltpu.SMEM((64,), jnp.int32),
+            pltpu.VMEM((1, 64), jnp.int32),
             pltpu.VMEM((1, 1, SLOTS, D), BF16),
             pltpu.VMEM((D, 4 * D), BF16),
             pltpu.VMEM((D, D), BF16),
@@ -507,11 +522,7 @@
 
 
 def local(histories, lengths, w_in, w_out, item_table, neg_blocks, targets):
-    blocks = neg_blocks[0]
-    rank = jnp.sum((blocks[None, :] < blocks[:, None]).astype(jnp.int32), axis=1)
-    places = jnp.arange(blocks.shape[0], dtype=jnp.int32)
-    order = jnp.sum(jnp.where(rank[:, None] == places[None, :], blocks[:, None], 0), axis=0)
-    value, loss, own = main(lengths, order, histories, w_in, w_out, item_table, targets)
+    value, loss, own = main(lengths, neg_blocks, histories, w_in, w_out, item_table, targets)
     item_grad, loss = finish(own, value, loss)
     return (loss[None], item_grad)
 

time: 61.7 us -> 60.1 us (0.974)
  other arithmetic: 2.18 us -> 0 us
    reduce_sum x2 -> x0, other arithmetic: 2.18 us -> none  [the longest x1 1.27 us: local(): jnp.sum(jnp.where(rank[:, None] == places[None, :], blocks[:, None], 0),...]
where the time goes in v4:
time: 60.1 us; the launch traced here: 59.9 us
  Pallas kernels  59.1 us (98%)
  between operations  0.8 us (1%)
    pallas_call x1, Pallas kernels, main(): pl.pallas_call(main_kernel, out_shape=(jax.ShapeDtypeStruct((CAND, D), F3...  56.9 us
    pallas_call x1, Pallas kernels, finish(): pl.pallas_call(finish_kernel, out_shape=(jax.ShapeDtypeStruct((16 * BLOCK...  2.23 us

profile of v4, /device:TPU:2, one launch (start us, length us, event | category | flops | bytes accessed | tf_op | source)
XLA Modules:
  0.0 59.9 jit_solution(5844058001052965774)
XLA Ops:
  0.6 56.9 %main.1 = (f32[512,256]{1,0:T(8,128)}, f32[1,512]{1,0:T(1,128)}, s32[8,128]{1,0:T(8,128)}) custom-call(s32[1,1,4]{2,1,0:T(1,128)} %len_hbm.1, s32[1,64]{1,0:T(1,128)} %neg_hbm.1, bf16[1,1,1024,256]{3,2,1,0:T(8,128)(2,1)} %hist_hbm.1, bf16[256,1024]{1,0:T(8,128)(2,1)} %win_hbm.1, bf16[256,256]{1,0:T(8,128)(2,1)} %wout_hbm.1, f32[2048,256]{1,0:T(8,128)} %table_hbm.1, ...), custom_call_target="tpu_custom_call" | custom-call | tf_op jit(solution)/shard_map/main/pallas_call | solution.py:417
  57.6 2.2 %finish.1 = (f32[2048,256]{1,0:T(8,128)}, f32[1,512]{1,0:T(1,128)}) custom-call(s32[8,128]{1,0:T(8,128)} %get-tuple-element.7.own_hbm, f32[512,256]{1,0:T(8,128)} %get-tuple-element.8.value_hbm, f32[1,512]{1,0:T(1,128)} %get-tuple-element.9.loss_in), custom_call_target="tpu_custom_call" | custom-call | tf_op jit(solution)/shard_map/finish/pallas_call | solution.py:506

commit v5 on v4

--- a/solution.py
+++ b/solution.py
@@ -21,7 +21,7 @@
 CAND = 512
 SCALE = 20.0
 EARLY = 1
-ARRIVE = ((1, 0), (3, 0), (1, 1), (3, 1), (2, 0), (2, 1))
+ARRIVE = ((1, 0), (3, 1), (1, 1), (3, 0), (2, 0), (2, 1))
 HALF = TOK // 2
 FAR_FIRST = (8, 9, 7, 10, 6, 11, 5, 12, 4, 13, 3, 14, 2, 15, 1)
 NEAR_FIRST = FAR_FIRST[::-1]
@@ -72,6 +72,7 @@
     grecv,
     hits,
     grad_ref,
+    value_ref,
     raw_ref,
     begin_ref,
     loss_ref,
@@ -283,24 +284,30 @@
         begin = second + tot[w + 1, 0:1, :]
     gather = jnp.concatenate(pieces, axis=1)
     pltpu.make_async_copy(recv.at[pl.ds(0, GROUP - 1)], recv.at[pl.ds(0, GROUP - 1)], a2a_r).wait()
-    own_tok = jnp.dot(gather, recv[...].reshape(GROUP * PAIR, D), preferred_element_type=F32).astype(BF16)
-    tok[2 * my_t] = own_tok[:HALF]
-    tok[2 * my_t + 1] = own_tok[HALF:]
-
-    tok_copies = {
-        (s, h): remote(
-            tok.at[2 * my_t + h], tok.at[2 * my_t + h], tok_s.at[2 * s + h], tok_r.at[2 * s + h], tok_peer(s)
-        )
-        for s, h in ARRIVE
-    }
-    for key in ARRIVE:
-        tok_copies[key].start()
+    received = recv[...].reshape(GROUP * PAIR, D)
+    tok_copies = {}
+    for h in (0, 1):
+        half = jnp.dot(gather[h * HALF : (h + 1) * HALF], received, preferred_element_type=F32)
+        tok[2 * my_t + h] = half.astype(BF16)
+        for s in ((1,), (3, 1, 3))[h]:
+            part_h = 0 if (s, h) in tok_copies else h
+            slot_h = tok.at[2 * my_t + part_h]
+            at = 2 * s + part_h
+            tok_copies[s, part_h] = remote(slot_h, slot_h, tok_s.at[at], tok_r.at[at], tok_peer(s))
+            tok_copies[s, part_h].start()
     for copy in cand_copies:
         copy.wait_recv()
 
     part = jnp.zeros((8, TOK), F32)
     for s, h in ((0, 0), (0, 1)) + ARRIVE:
-        if s:
+        if (s, h) == (1, 0):
+            for near_s, near_h in ((1, 0), (3, 1)):
+                tok_copies[near_s, near_h].wait_recv()
+                slot_h = tok.at[2 * lax.rem(my_t + SIDE - near_s, SIDE) + near_h]
+                at = 4 + near_h
+                tok_copies[2, near_h] = remote(slot_h, slot_h, tok_s.at[at], tok_r.at[at], tok_peer(near_s))
+                tok_copies[2, near_h].start()
+        elif s and (s, h) != (3, 1):
             tok_copies[s, h].wait_recv()
         t = lax.rem(my_t + SIDE - s, SIDE)
 
@@ -339,38 +346,32 @@
     sumexp = (sums[0] + sums[1]) + (sums[2] + sums[3])
     inverse = 1.0 / sumexp
 
-    g_copies = []
+    g_copies = {}
     part = jnp.zeros((8, TOK), F32)
-    for s in (2, 1, 3, 0):
+    for half, s in ((0, 2), (0, 1), (0, 3), (1, 2), (1, 1), (1, 3), (0, 0), (1, 0)):
         c = lax.rem(my_c + s, SIDE)
-        for half in range(2):
-            total = jnp.zeros((2 * BLOCK, D), F32)
-            for t in range(SIDE):
-                target = target_of(t)
-                scale_t = inverse[t : t + 1, :]
-                slopes = []
-                found = jnp.zeros((8, TOK), F32)
-                for q in (2 * half, 2 * half + 1):
-                    value = expd[t, pl.ds(pl.multiple_of(c * CAND + q * BLOCK, BLOCK), BLOCK), :]
-                    hit = offset == target - starts[s, q]
-                    slopes.append((value * scale_t - jnp.where(hit, 1.0, 0.0)).astype(BF16))
-                    found = found + jnp.sum(jnp.where(hit, value, 0.0).reshape(BLOCK // 8, 8, TOK), axis=0)
-                total = total + jnp.dot(jnp.concatenate(slopes, axis=0), tok[2 * t : 2 * t + 2].reshape(TOK, D), preferred_element_type=F32)
-                part = part + jnp.where(row8 == t, jnp.sum(found, axis=0, keepdims=True), 0.0)
-            rows = pl.ds(half * 2 * BLOCK, 2 * BLOCK)
-            if s:
-                gsend[2 * s + half] = (SCALE * total).astype(BF16)
-                copy = remote(
-                    gsend.at[2 * s + half],
-                    grecv.at[2 * s + half],
-                    g_s.at[2 * s + half],
-                    g_r.at[2 * s + half],
-                    cand_peer(s),
-                )
-                copy.start()
-                g_copies.append(copy)
-            else:
-                grad_ref[rows, :] = SCALE * total
+        total = jnp.zeros((2 * BLOCK, D), F32)
+        for t in range(SIDE):
+            target = target_of(t)
+            scale_t = inverse[t : t + 1, :]
+            slopes = []
+            found = jnp.zeros((8, TOK), F32)
+            for q in (2 * half, 2 * half + 1):
+                value = expd[t, pl.ds(pl.multiple_of(c * CAND + q * BLOCK, BLOCK), BLOCK), :]
+                hit = offset == target - starts[s, q]
+                slopes.append((value * scale_t - jnp.where(hit, 1.0, 0.0)).astype(BF16))
+                found = found + jnp.sum(jnp.where(hit, value, 0.0).reshape(BLOCK // 8, 8, TOK), axis=0)
+            both = tok[2 * t : 2 * t + 2].reshape(TOK, D)
+            total = total + jnp.dot(jnp.concatenate(slopes, axis=0), both, preferred_element_type=F32)
+            part = part + jnp.where(row8 == t, jnp.sum(found, axis=0, keepdims=True), 0.0)
+        if s:
+            at = 2 * s + half
+            gsend[at] = (SCALE * total).astype(BF16)
+            copy = remote(gsend.at[at], grecv.at[at], g_s.at[at], g_r.at[at], cand_peer(s))
+            copy.start()
+            g_copies[s, half] = copy
+        else:
+            grad_ref[half] = SCALE * total
     hits[my_t] = part
     hit_copies = [
         remote(hits.at[my_t], hits.at[my_t], hit_s.at[s], hit_r.at[s], tok_peer(s)) for s in range(1, SIDE)
@@ -388,23 +389,21 @@
     ]
     for copy in outs:
         copy.start()
-    for q in range(4):
-        if q % 2 == 0:
-            for s in range(3):
-                g_copies[2 * s + q // 2].wait_recv()
-        at = pl.ds(q * BLOCK, BLOCK)
-        part = pl.ds(q % 2 * BLOCK, BLOCK)
-        grad = (grad_ref[at, :] + grecv[2 + q // 2, part, :].astype(F32)) + (
-            grecv[4 + q // 2, part, :].astype(F32) + grecv[6 + q // 2, part, :].astype(F32)
+    for half in range(2):
+        for s in range(1, SIDE):
+            g_copies[s, half].wait_recv()
+        grad = (grad_ref[half] + grecv[2 + half].astype(F32)) + (
+            grecv[4 + half].astype(F32) + grecv[6 + half].astype(F32)
         )
+        at = pl.ds(half * HALF, HALF)
         rows = raw_ref[at, :]
         scale = unit_scale(rows)
         along = jnp.mean(rows * grad, axis=-1, keepdims=True)
-        grad_ref[at, :] = (grad - rows * (scale * scale * along)) * (scale * 0.0625)
-    outs.append(pltpu.make_async_copy(grad_ref, value_hbm, out_s.at[0]))
-    outs[-1].start()
-
-    for copy in tot_copies + cand_copies + list(tok_copies.values()) + sum_copies + hit_copies + g_copies:
+        value_ref[half] = (grad - rows * (scale * scale * along)) * (scale * 0.0625)
+        outs.append(pltpu.make_async_copy(value_ref.at[half], value_hbm.at[at], out_s.at[3 * half]))
+        outs[-1].start()
+
+    for copy in tot_copies + cand_copies + list(tok_copies.values()) + sum_copies + hit_copies + list(g_copies.values()):
         copy.wait_send()
     for copy in outs:
         copy.wait()
@@ -445,11 +444,12 @@
             pltpu.VMEM((2 * SIDE, HALF, D), BF16),
             pltpu.VMEM((2 * SIDE, HALF, D), BF16),
             pltpu.VMEM((SIDE, 8, TOK), F32),
-            pltpu.VMEM((CAND, D), F32),
+            pltpu.VMEM((2, HALF, D), F32),
+            pltpu.VMEM((2, HALF, D), F32),
             pltpu.VMEM((CAND, D), F32),
             pltpu.VMEM((8, 128), jnp.int32),
             pltpu.VMEM((1, TOK), F32),
-            dma((3,)),
+            dma((4,)),
             dma((7,)),
             dma((GROUP,)),
             dma((GROUP,)),

time: 60.1 us -> 59.4 us (0.988)
  Pallas kernels: 59.1 us -> 58.4 us
    pallas_call x1, Pallas kernels: 56.9 us -> 56.2 us  [main(): pl.pallas_call(main_kernel, out_shape=(jax.ShapeDtypeStruct((CAND, D), F3...]
where the time goes in v5:
time: 59.4 us; the launch traced here: 59.2 us
  Pallas kernels  58.4 us (98%)
  between operations  0.8 us (1%)
    pallas_call x1, Pallas kernels, main(): pl.pallas_call(main_kernel, out_shape=(jax.ShapeDtypeStruct((CAND, D), F3...  56.2 us
    pallas_call x1, Pallas kernels, finish(): pl.pallas_call(finish_kernel, out_shape=(jax.ShapeDtypeStruct((16 * BLOCK...  2.23 us

profile of v5, /device:TPU:2, one launch (start us, length us, event | category | flops | bytes accessed | tf_op | source)
XLA Modules:
  0.0 59.2 jit_solution(10936434836105170351)
XLA Ops:
  0.6 56.2 %main.1 = (f32[512,256]{1,0:T(8,128)}, f32[1,512]{1,0:T(1,128)}, s32[8,128]{1,0:T(8,128)}) custom-call(s32[1,1,4]{2,1,0:T(1,128)} %len_hbm.1, s32[1,64]{1,0:T(1,128)} %neg_hbm.1, bf16[1,1,1024,256]{3,2,1,0:T(8,128)(2,1)} %hist_hbm.1, bf16[256,1024]{1,0:T(8,128)(2,1)} %win_hbm.1, bf16[256,256]{1,0:T(8,128)(2,1)} %wout_hbm.1, f32[2048,256]{1,0:T(8,128)} %table_hbm.1, ...), custom_call_target="tpu_custom_call" | custom-call | tf_op jit(solution)/shard_map/main/pallas_call | solution.py:416
  56.8 2.2 %finish.1 = (f32[2048,256]{1,0:T(8,128)}, f32[1,512]{1,0:T(1,128)}) custom-call(s32[8,128]{1,0:T(8,128)} %get-tuple-element.7.own_hbm, f32[512,256]{1,0:T(8,128)} %get-tuple-element.8.value_hbm, f32[1,512]{1,0:T(1,128)} %get-tuple-element.9.loss_in), custom_call_target="tpu_custom_call" | custom-call | tf_op jit(solution)/shard_map/finish/pallas_call | solution.py:506
